TPU v7x, 32 devices: a whole 2x2x4 slice. The times are simulated.
32 devices in a mesh: dp: 16 (over z, y, x), seq: 2 (over core).
Axes of the slice: x: 2, y: 2, z: 4, core: 2. Of those that a mesh axis runs over, the one named last changes fastest.
Arguments:
- latents: float32 [16, 512, 1024], P('dp', 'seq'), may hold values from -6 to 6
- pixels: float32 [16, 8192, 261], P('dp', 'seq'), may hold values from -6 to 6
- keep_mask: int32 [16, 8192], P('dp', 'seq'), may hold values from 0 to 1, as said below
- cotangent: float32 [16, 512, 1024], P('dp', 'seq'), may hold values from -6 to 6
- square_weights: float32 [4, 1024, 1024], P(None, None, 'dp')
- square_first: float32 [4, 1024, 1024], P(None, None, 'dp')
- square_second: float32 [4, 1024, 1024], P(None, None, 'dp')
- pixel_weights: float32 [2, 261, 1024], P(None, None, 'dp')
- pixel_first: float32 [2, 261, 1024], P(None, None, 'dp')
- pixel_second: float32 [2, 261, 1024], P(None, None, 'dp')
- latent_vectors: float32 [6, 1024], replicated
- latent_first: float32 [6, 1024], replicated
- latent_second: float32 [6, 1024], replicated
- pixel_norm: float32 [2, 261], replicated
- pixel_norm_first: float32 [2, 261], replicated
- pixel_norm_second: float32 [2, 261], replicated
Outputs:
- latents_out: float32 [16, 512, 1024], P('dp', 'seq')
- latents_grad: float32 [16, 512, 1024], P('dp', 'seq')
- pixels_grad: float32 [16, 8192, 261], P('dp', 'seq')
- square_grad: float32 [4, 1024, 1024], P(None, None, 'dp')
- square_first_new: float32 [4, 1024, 1024], P(None, None, 'dp')
- square_second_new: float32 [4, 1024, 1024], P(None, None, 'dp')
- square_new: float32 [4, 1024, 1024], P(None, None, 'dp')
- square_half: bfloat16 [4, 1024, 1024], P(None, None, 'dp')
- pixel_weight_grad: float32 [2, 261, 1024], P(None, None, 'dp')
- pixel_first_new: float32 [2, 261, 1024], P(None, None, 'dp')
- pixel_second_new: float32 [2, 261, 1024], P(None, None, 'dp')
- pixel_new: float32 [2, 261, 1024], P(None, None, 'dp')
- pixel_half: bfloat16 [2, 261, 1024], P(None, None, 'dp')
- latent_first_new: float32 [6, 1024], replicated
- latent_second_new: float32 [6, 1024], replicated
- latent_vectors_new: float32 [6, 1024], replicated
- pixel_norm_first_new: float32 [2, 261], replicated
- pixel_norm_second_new: float32 [2, 261], replicated
- pixel_norm_new: float32 [2, 261], replicated
- matrix_norms: float32 [3, 6], replicated
Inputs may be any that keep to these rules, and one draw needn't show every extreme that they name: keep_mask[i, 0] = 1 for every image i; each image drops its other pixels with a share drawn for it between 10 and 60 percent.
All inputs are finite; a program needn't handle non-finite values.
Results may differ from a plain program's by a relative error of at most 0.015.
The roundings to bfloat16 on the way count: a program that leaves them out, or rounds other values in their place, can miss the bound.
Values may be sent and summed in bfloat16 or wider, within the bound.
No kernel may reach another device: no remote copies, remote signals or barrier semaphores. Data moves between devices by JAX's collectives and lax.ppermute only.
A program may use at most 320 MiB of HBM per device.

v0:
```python
import functools

import jax
import jax.numpy as jnp
from jax import lax
from jax.experimental import pallas as pl
from jax.experimental.pallas import tpu as pltpu
from jax.sharding import PartitionSpec as P

STEP = 10


norm_epsilon = 1e-05
beta_one = 0.9
beta_two = 0.999
decay_rate = 0.01
epsilon = 1e-06
learn_rate = 0.25
vector_rate = 1.0
masked_score = -1e30
gelu_coeff = 0.7978845608028654


def adam_moments(grad, first, second):
    first_new = beta_one * first + (1.0 - beta_one) * grad
    second_new = beta_two * second + (1.0 - beta_two) * grad * grad
    ratio = (
        first_new
        / (1.0 - beta_one**STEP)
        / (jnp.sqrt(second_new / (1.0 - beta_two**STEP)) + epsilon)
    )
    return (first_new, second_new, ratio)

half = jnp.bfloat16
single = jnp.float32
swap = [(0, 1), (1, 0)]
main, rest = 256, 128
whole = pl.BlockSpec(memory_space=pltpu.VMEM)
remote = pl.BlockSpec(memory_space=pl.ANY)
scalars = pl.BlockSpec(memory_space=pltpu.SMEM)
params = pltpu.CompilerParams(vmem_limit_bytes=56 * 2**20)


def shape(dims, dtype):
    return jax.ShapeDtypeStruct(dims, dtype)


def contract(left, right, over_left, over_right):
    return lax.dot_general(left, right, (((over_left,), (over_right,)), ((), ())), preferred_element_type=single)


def nn(left, right):
    return contract(left, right, 1, 0)


def nt(left, right):
    return contract(left, right, 1, 1)


def tn(left, right):
    return contract(left, right, 0, 0)


def flip(array, mask):
    return lax.ppermute(array, "dp", [(i, i ^ mask) for i in range(lax.axis_size("dp"))])


def trade(array):
    return lax.ppermute(array, "seq", swap)


def special(groups, shard):
    return groups == 16 and shard % 32 == 0


def gather_blocks(block):
    got = [None] * 16
    got[0] = block
    got[8] = flip(got[0], 8)
    got[4] = flip(got[0], 4)
    got[1] = flip(got[0], 1)
    got[2] = flip(got[0], 2)
    got[3] = flip(got[2], 1)
    got[12] = flip(got[8], 4)
    got[5] = flip(got[4], 1)
    got[6] = flip(got[4], 2)
    got[9] = flip(got[8], 1)
    got[10] = flip(got[8], 2)
    got[7] = flip(got[5], 2)
    got[11] = flip(got[10], 1)
    got[13] = flip(got[12], 1)
    got[14] = flip(got[12], 2)
    got[15] = flip(got[13], 2)
    return got


def gather_matrices(squares, pixel):
    matrices, shard, width = squares.shape
    part = width // 2
    core = lax.axis_index("seq")
    groups = lax.axis_size("dp")
    block = jnp.concatenate(
        [lax.dynamic_slice_in_dim(squares[m], core * part, part, 1) for m in range(matrices)]
        + [lax.dynamic_slice_in_dim(pixel, core * main, main, 1)],
        axis=1,
    )
    if special(groups, shard):
        blocks = []
        for got in gather_blocks(block):
            blocks += [got, trade(got)]
        return blocks
    every = lax.all_gather(block, ("dp", "seq"), axis=0).reshape(groups, 2, shard, -1)
    return [every.transpose(1, 0, 2, 3).reshape(2, groups * shard, -1)]


def load_blocks(spot, blocks, target, sems):
    copies = []
    if len(blocks) == 1:
        copies.append(pltpu.make_async_copy(blocks[0], target, sems.at[0]))
    else:
        for i, block in enumerate(blocks):
            rows = block.shape[0]
            chip = lax.bitwise_xor(spot[0], i // 2)
            side = lax.bitwise_xor(spot[1], i % 2)
            place = target.at[side, pl.ds(pl.multiple_of(chip * rows, rows), rows)]
            copies.append(pltpu.make_async_copy(block, place, sems.at[i]))
    for copy in copies:
        copy.start()
    return copies


def store_terms(spot, terms, outs):
    if len(outs) == 1:
        outs[0][...] = terms[...].astype(half)
        return
    send_a, keep_a, send_b, keep_b = outs
    rows = terms.shape[0] // 16
    for o in range(16):
        chip = lax.bitwise_xor(spot[0], o)
        upper = terms[pl.ds(pl.multiple_of(chip * rows, rows), rows // 2), :].astype(half)
        lower = terms[pl.ds(pl.multiple_of(chip * rows + rows // 2, rows // 2), rows // 2), :].astype(half)
        (send_a if o & 1 else keep_a)[o // 2] = upper
        (send_b if o & 2 else keep_b)[(o // 4) * 2 + o % 2] = lower


def term_shapes(groups, shard, lanes):
    if special(groups, shard):
        return [shape((8, shard // 2, lanes), half)] * 4
    return [shape((groups * shard, lanes), half)]


def scatter_sum(terms, groups):
    if len(terms) == 1:
        return lax.psum_scatter(terms[0], "dp", scatter_dimension=0, tiled=True).astype(single)
    send_a, keep_a, send_b, keep_b = terms

    def split(array):
        array = array.reshape(-1, 2, *array.shape[1:])
        return array[:, 0], array[:, 1].astype(half)

    def add(kept, got):
        return kept.astype(single) + got.astype(single)

    a, b = add(keep_a, flip(send_a, 1)), add(keep_b, flip(send_b, 2))
    (keep_a, send_a), (keep_b, send_b) = split(a), split(b)
    a, b = add(keep_a, flip(send_a, 2)), add(keep_b, flip(send_b, 1))
    held = jnp.concatenate([a, b], axis=1)
    kept, sent = split(held)
    held = add(kept, flip(sent, 4))
    kept, sent = split(held)
    return add(kept, flip(sent, 8))[0]


def sum_all(array, seq):
    if seq:
        array = array + trade(array)
    mask = 1
    size = lax.axis_size("dp")
    while mask < size:
        if mask * 2 < size:
            one, two, three = flip(array, mask), flip(array, 2 * mask), flip(array, 3 * mask)
            array = (array + one) + (two + three)
            mask *= 4
        else:
            array = array + flip(array, mask)
            mask *= 2
    return array


def standard(values):
    center = values - jnp.mean(values, axis=-1, keepdims=True)
    inverse = lax.rsqrt(jnp.mean(center * center, axis=-1, keepdims=True) + norm_epsilon)
    return center * inverse, inverse


def standard_back(grad, gain, unit, inverse):
    scaled = grad * gain
    return inverse * (
        scaled - jnp.mean(scaled, axis=-1, keepdims=True) - unit * jnp.mean(scaled * unit, axis=-1, keepdims=True)
    )


def pixel_kernel(pixels, gain, shift, normed, stats, held, tail, sem):
    copy = pltpu.make_async_copy(pixels.at[:, 0, :], held, sem)
    copy.start()
    feats = held.shape[0]
    step = 256
    over = feats - main
    tail[...] = jnp.zeros_like(tail)
    copy.wait()

    @pl.loop(0, held.shape[1] // step)
    def _(i):
        lanes = pl.ds(pl.multiple_of(i * step, step), step)
        first, last = held[pl.ds(0, main), lanes], held[pl.ds(main, over), lanes]
        mean = (jnp.sum(first, axis=0, keepdims=True) + jnp.sum(last, axis=0, keepdims=True)) / feats
        first, last = first - mean, last - mean
        spread = (
            jnp.sum(first * first, axis=0, keepdims=True) + jnp.sum(last * last, axis=0, keepdims=True)
        ) / feats
        inverse = lax.rsqrt(spread + norm_epsilon)
        normed[pl.ds(0, main), lanes] = (first * inverse * gain[pl.ds(0, main)] + shift[pl.ds(0, main)]).astype(half)
        tail[pl.ds(0, over), :] = last * inverse * gain[pl.ds(main, over)] + shift[pl.ds(main, over)]
        normed[pl.ds(main, rest), lanes] = tail[...].astype(half)
        stats[0:1, lanes] = mean
        stats[1:2, lanes] = inverse


def norm_pixels(pixels, gain, shift):
    feats, _, count = pixels.shape
    return pl.pallas_call(
        pixel_kernel,
        out_shape=[shape((main + rest, count), half), shape((2, count), single)],
        in_specs=[remote, whole, whole],
        out_specs=[whole] * 2,
        scratch_shapes=[pltpu.VMEM((feats, count), single), pltpu.VMEM((rest, 256), single), pltpu.SemaphoreType.DMA],
        compiler_params=params,
        name="norm_pixels",
    )(pixels, gain, shift)


def latent_kernel(mine, theirs, vectors, normed):
    for t, source in enumerate((mine, theirs)):
        rows = source.shape[0]
        unit, _ = standard(source[...])
        normed[pl.ds(t * rows, rows), :] = (unit * vectors[0:1, :] + vectors[1:2, :]).astype(half)


def norm_latents(mine, theirs, vectors):
    return pl.pallas_call(
        latent_kernel,
        out_shape=shape((2 * mine.shape[0], mine.shape[1]), half),
        in_specs=[whole] * 3,
        out_specs=whole,
        compiler_params=params,
        name="norm_latents",
    )(mine, theirs, vectors)


def attend_kernel(count, scale, feats, spot, *refs):
    blocks = refs[:count]
    normed, pixels, keep, query, query_pix, sent, weights, sems = refs[count:]
    copies = load_blocks(spot, blocks, weights, sems)
    for copy in copies:
        copy.wait()
    part = normed.shape[1] // 2
    step = 256
    for t in range(normed.shape[0] // step):
        rows = pl.ds(t * step, step)
        value = nt(normed[rows, pl.ds(0, part)], weights[0, :, pl.ds(0, part)])
        value = value + nt(normed[rows, pl.ds(part, part)], weights[1, :, pl.ds(0, part)])
        value = value.astype(half)
        query[rows, :] = value
        query_pix[rows, pl.ds(0, main)] = (nn(value, weights[0, :, pl.ds(part, main)]) * scale).astype(half)
        query_pix[rows, pl.ds(main, rest)] = (nn(value, weights[1, :, pl.ds(part, rest)]) * scale).astype(half)
    tile = 128

    @pl.loop(0, normed.shape[0] // tile)
    def _(i):
        rows = pl.ds(pl.multiple_of(i * tile, tile), tile)
        scores = nn(query_pix[rows, pl.ds(0, main)], pixels[pl.ds(0, main), :])
        scores = scores + nn(query_pix[rows, pl.ds(main, rest)], pixels[pl.ds(main, rest), :])
        scores = jnp.where(keep[...] > 0, scores, masked_score)
        top = jnp.max(scores, axis=-1, keepdims=True)
        expo = jnp.exp(scores - top)
        total = jnp.sum(expo, axis=-1, keepdims=True)
        expo = expo.astype(half)
        sent[rows, pl.ds(0, main)] = nt(expo, pixels[pl.ds(0, main), :])
        last = nt(expo, pixels[pl.ds(main, rest), :])
        lane = lax.broadcasted_iota(jnp.int32, last.shape, 1)
        last = jnp.where(lane == feats - main, top, jnp.where(lane == feats - main + 1, total, last))
        sent[rows, pl.ds(main, rest)] = last


def attend(spot, blocks, normed, pixels, keep, scale, feats):
    rows, width = normed.shape
    lanes = blocks[0].shape[-1]
    return pl.pallas_call(
        functools.partial(attend_kernel, len(blocks), scale, feats),
        out_shape=[shape((rows, width), half), shape((rows, main + rest), half), shape((rows, main + rest), single)],
        in_specs=[scalars] + [remote] * len(blocks) + [whole] * 3,
        out_specs=[whole] * 3,
        scratch_shapes=[pltpu.VMEM((2, width, lanes), half), pltpu.SemaphoreType.DMA((len(blocks),))],
        compiler_params=params,
        name="attend",
    )(spot, *blocks, normed, pixels, keep)


def chain_kernel(count, terms_count, feats, spot, *refs):
    blocks, refs = refs[:count], refs[count:]
    (mine, theirs, latent_mine, latent_theirs, cot_mine, cot_theirs, vectors), refs = refs[:7], refs[7:]
    (latents_out, middle_grad, grad_pix, stats, sums), refs = refs[:5], refs[5:]
    term_outs, refs = refs[:terms_count], refs[terms_count:]
    weights, attended, middle_half, mixed, hidden_grad, active, out_half, attended_grad, value_mix, wide, terms, sems = refs
    copies = load_blocks(spot, blocks, weights, sems)
    for copy in copies:
        copy.wait()
    rows_all, width = attended.shape
    step = rows_all // 2
    part = width // 2

    def into(value, m):
        lanes = pl.ds(m * part, part)
        return nt(value[:, :part], weights[0, :, lanes]) + nt(value[:, part:], weights[1, :, lanes])

    def back(value, m, target):
        lanes = pl.ds(m * part, part)
        target[:, pl.ds(0, part)] = nn(value, weights[0, :, lanes])
        target[:, pl.ds(part, part)] = nn(value, weights[1, :, lanes])
        return target[...]

    sums[...] = jnp.zeros_like(sums)
    value_mix[...] = jnp.zeros_like(value_mix)
    for t in range(2):
        rows, other = pl.ds(t * step, step), pl.ds((1 - t) * step, step)
        latents, cotangent = (latent_mine, cot_mine) if t == 0 else (latent_theirs, cot_theirs)
        here, there = mine[rows, :], theirs[other, :]
        top_here, top_there = here[:, feats : feats + 1], there[:, feats : feats + 1]
        top = jnp.maximum(top_here, top_there)
        scale_here, scale_there = jnp.exp(top_here - top), jnp.exp(top_there - top)
        total = here[:, feats + 1 : feats + 2] * scale_here + there[:, feats + 1 : feats + 2] * scale_there
        mix = (here * scale_here + there * scale_there) / total
        lane = lax.broadcasted_iota(jnp.int32, mix.shape, 1)
        mix = jnp.where(lane < feats, mix, 0.0).astype(half)
        value_mix[rows, pl.ds(0, main + rest)] = mix
        attended_f = nt(mix[:, :main], weights[0, :, pl.ds(3 * part, main)])
        attended_f = attended_f + nt(mix[:, main:], weights[1, :, pl.ds(3 * part, rest)])
        wide[...] = attended_f
        value = attended_f.astype(half)
        attended[rows, :] = value
        middle = latents[...] + into(value, 0)
        unit, inverse = standard(middle)
        value = (unit * vectors[2:3, :] + vectors[3:4, :]).astype(half)
        mixed[rows, :] = value
        hidden = into(value, 1) + vectors[4:5, :]
        curve = jnp.tanh(gelu_coeff * (hidden + 0.044715 * hidden * hidden * hidden))
        value = (0.5 * hidden * (1.0 + curve)).astype(half)
        active[rows, :] = value
        if t == 0:
            latents_out[...] = middle + into(value, 2) + vectors[5:6, :]
        slope = 0.5 * (1.0 + curve) + 0.5 * hidden * (1.0 - curve * curve) * gelu_coeff * (
            1.0 + 3.0 * 0.044715 * hidden * hidden
        )
        value = cotangent[...].astype(half)
        out_half[rows, :] = value
        if t == 0:
            sums[5:6, :] = jnp.sum(value.astype(single), axis=0, keepdims=True)
        scratch = terms.at[pl.ds(0, step), pl.ds(0, width)]
        value = (back(value, 2, scratch) * slope).astype(half)
        hidden_grad[rows, :] = value
        if t == 0:
            sums[4:5, :] = jnp.sum(value.astype(single), axis=0, keepdims=True)
        mixed_grad = back(value, 1, scratch)
        if t == 0:
            sums[2:3, :] = jnp.sum(mixed_grad * unit, axis=0, keepdims=True)
            sums[3:4, :] = jnp.sum(mixed_grad, axis=0, keepdims=True)
        grad = cotangent[...] + standard_back(mixed_grad, vectors[2:3, :], unit, inverse)
        if t == 0:
            middle_grad[...] = grad
        value = grad.astype(half)
        middle_half[rows, :] = value
        value = back(value, 0, scratch).astype(half)
        attended_grad[rows, :] = value
        inner = jnp.sum(wide[...] * value.astype(single), axis=-1, keepdims=True)
        grad_pix[rows, pl.ds(0, main)] = nn(value, weights[0, :, pl.ds(3 * part, main)]).astype(half)
        grad_pix[rows, pl.ds(main, rest)] = nn(value, weights[1, :, pl.ds(3 * part, rest)]).astype(half)
        lane = lax.broadcasted_iota(jnp.int32, (step, 128), 1)
        stats[rows, :] = jnp.where(lane == 0, top + jnp.log(total), inner)
    side = pl.ds(pl.multiple_of(spot[1] * part, part), part)
    for m, (grad, value) in enumerate(((middle_half, attended), (hidden_grad, mixed), (out_half, active))):
        terms[:, pl.ds(m * part, part)] = tn(grad[...], value[:, side])
    side = pl.ds(pl.multiple_of(spot[1] * main, main), main)
    terms[:, pl.ds(3 * part, main)] = tn(attended_grad[...], value_mix[:, side])
    store_terms(spot, terms, term_outs)


def chain(spot, blocks, mine, theirs, latents, cotangents, vectors, feats, groups):
    rows, width = mine.shape[0], vectors.shape[1]
    lanes = blocks[0].shape[-1]
    outs = term_shapes(groups, width // groups, lanes)
    bits = pltpu.VMEM((rows, width), half)
    result = pl.pallas_call(
        functools.partial(chain_kernel, len(blocks), len(outs), feats),
        out_shape=[
            shape((rows // 2, width), single),
            shape((rows // 2, width), single),
            shape((rows, main + rest), half),
            shape((rows, 128), single),
            shape((8, width), single),
        ]
        + outs,
        in_specs=[scalars] + [remote] * len(blocks) + [whole] * 7,
        out_specs=[whole] * (5 + len(outs)),
        scratch_shapes=[pltpu.VMEM((2, width, lanes), half)]
        + [bits] * 7
        + [
            pltpu.VMEM((rows, 2 * main), half),
            pltpu.VMEM((rows // 2, width), single),
            pltpu.VMEM((width, lanes), single),
            pltpu.SemaphoreType.DMA((len(blocks),)),
        ],
        compiler_params=params,
        name="chain",
    )(spot, *blocks, mine, theirs, *latents, *cotangents, vectors)
    return result[:5], result[5:]


def pixel_back_kernel(
    scale, query_pix, grad_pix, stats, normed, keep, pixels, gain, pixel_stats, score_pix, pixels_grad, sums, held, made, query_t, grad_t, slope, shift, sem, sems
):
    copy = pltpu.make_async_copy(pixels.at[:, 0, :], held, sem)
    copy.start()
    feats, count = held.shape
    over = feats - main
    step = 512
    query_t[...] = jnp.transpose(query_pix[...].astype(single)).astype(half)
    grad_t[...] = jnp.transpose(grad_pix[...].astype(single)).astype(half)
    score_pix[...] = jnp.zeros_like(score_pix)
    slope[...] = jnp.zeros_like(slope)
    shift[...] = jnp.zeros_like(shift)
    log_total, inner = stats[:, 0:1], stats[:, 1:2]
    copy.wait()

    @pl.loop(0, count // step)
    def _(i):
        lanes = pl.ds(pl.multiple_of(i * step, step), step)
        first, last = normed[pl.ds(0, main), lanes], normed[pl.ds(main, rest), lanes]
        scores = nn(query_pix[:, pl.ds(0, main)], first) + nn(query_pix[:, pl.ds(main, rest)], last)
        weight_grad = nn(grad_pix[:, pl.ds(0, main)], first) + nn(grad_pix[:, pl.ds(main, rest)], last)
        attn = jnp.exp(jnp.where(keep[:, lanes] > 0, scores, masked_score) - log_total)
        score_grad = (attn * (weight_grad - inner)).astype(half)
        attn = attn.astype(half)
        score_pix[:, pl.ds(0, main)] += nt(score_grad, first)
        score_pix[:, pl.ds(main, rest)] += nt(score_grad, last)
        grad = nn(query_t[...], score_grad) + nn(grad_t[...], attn)
        mean, inverse = pixel_stats[0:1, lanes], pixel_stats[1:2, lanes]
        unit_a = (held[pl.ds(0, main), lanes] - mean) * inverse
        unit_b = (held[pl.ds(main, over), lanes] - mean) * inverse
        grad_a, grad_b = grad[:main], grad[main : main + over]
        for rows, g, u in ((pl.ds(0, main), grad_a, unit_a), (pl.ds(main, over), grad_b, unit_b)):
            product = g * u
            slope[rows, :] += sum(product[:, 128 * j : 128 * j + 128] for j in range(step // 128))
            shift[rows, :] += sum(g[:, 128 * j : 128 * j + 128] for j in range(step // 128))
        scaled_a, scaled_b = grad_a * gain[pl.ds(0, main)], grad_b * gain[pl.ds(main, over)]
        flat = (jnp.sum(scaled_a, axis=0, keepdims=True) + jnp.sum(scaled_b, axis=0, keepdims=True)) / feats
        along = (
            jnp.sum(scaled_a * unit_a, axis=0, keepdims=True) + jnp.sum(scaled_b * unit_b, axis=0, keepdims=True)
        ) / feats
        made[pl.ds(0, main), lanes] = inverse * (scaled_a - flat - unit_a * along)
        made[pl.ds(main, over), lanes] = inverse * (scaled_b - flat - unit_b * along)
        pltpu.make_async_copy(made.at[:, lanes], pixels_grad.at[:, 0, lanes], sems.at[i]).start()

    score_pix[...] = score_pix[...] * scale
    lane = lax.broadcasted_iota(jnp.int32, (feats, 128), 1)
    sums[...] = jnp.where(
        lane == 0,
        jnp.sum(slope[...], axis=-1, keepdims=True),
        jnp.sum(shift[...], axis=-1, keepdims=True),
    )

    @pl.loop(0, count // step)
    def _(i):
        lanes = pl.ds(pl.multiple_of(i * step, step), step)
        pltpu.make_async_copy(made.at[:, lanes], pixels_grad.at[:, 0, lanes], sems.at[i]).wait()


def pixel_back(query_pix, grad_pix, stats, normed, keep, pixels, gain, pixel_stats, scale):
    feats, _, count = pixels.shape
    rows = query_pix.shape[0]
    big = pltpu.VMEM((feats, count), single)
    return pl.pallas_call(
        functools.partial(pixel_back_kernel, scale),
        out_shape=[shape((rows, main + rest), single), shape(pixels.shape, single), shape((feats, 128), single)],
        in_specs=[whole] * 5 + [remote, whole, whole],
        out_specs=[whole, remote, whole],
        scratch_shapes=[
            big,
            big,
            pltpu.VMEM((main + rest, rows), half),
            pltpu.VMEM((main + rest, rows), half),
            pltpu.VMEM((feats, 128), single),
            pltpu.VMEM((feats, 128), single),
            pltpu.SemaphoreType.DMA,
            pltpu.SemaphoreType.DMA((count // 512,)),
        ],
        compiler_params=params,
        name="pixel_back",
    )(query_pix, grad_pix, stats, normed, keep, pixels, gain, pixel_stats)


def query_back_kernel(count, terms_count, spot, *refs):
    blocks, refs = refs[:count], refs[count:]
    (mine, theirs, query, normed, latents, middle_grad, vectors), refs = refs[:7], refs[7:]
    (latents_grad, sums), refs = refs[:2], refs[2:]
    term_outs, refs = refs[:terms_count], refs[terms_count:]
    weights, score_pix, query_grad, wide, terms, sems = refs
    copies = load_blocks(spot, blocks, weights, sems)
    rows_all, width = query.shape
    step = rows_all // 2
    part = width // 2
    score_pix[:, pl.ds(main + rest, rest)] = jnp.zeros((rows_all, rest), half)
    for t in range(2):
        rows, other = pl.ds(t * step, step), pl.ds((1 - t) * step, step)
        score_pix[rows, pl.ds(0, main + rest)] = (mine[rows, :] + theirs[other, :]).astype(half)
    for copy in copies:
        copy.wait()
    for t in range(2):
        rows = pl.ds(t * step, step)
        value = nt(score_pix[rows, pl.ds(0, main)], weights[0, :, pl.ds(part, main)])
        value = value + nt(score_pix[rows, pl.ds(main, rest)], weights[1, :, pl.ds(part, rest)])
        query_grad[rows, :] = value.astype(half)
    side = pl.ds(pl.multiple_of(spot[1] * part, part), part)
    terms[:, pl.ds(0, part)] = tn(query_grad[...], normed[:, side])
    side = pl.ds(pl.multiple_of(spot[1] * main, main), main)
    terms[:, pl.ds(part, main)] = tn(query[...], score_pix[:, side])
    store_terms(spot, terms, term_outs)
    value = query_grad[pl.ds(0, step), :]
    wide[:, pl.ds(0, part)] = nn(value, weights[0, :, pl.ds(0, part)])
    wide[:, pl.ds(part, part)] = nn(value, weights[1, :, pl.ds(0, part)])
    unit, inverse = standard(latents[...])
    grad = wide[...]
    latents_grad[...] = middle_grad[...] + standard_back(grad, vectors[0:1, :], unit, inverse)
    sums[...] = jnp.zeros_like(sums)
    sums[0:1, :] = jnp.sum(grad * unit, axis=0, keepdims=True)
    sums[1:2, :] = jnp.sum(grad, axis=0, keepdims=True)


def query_back(spot, blocks, mine, theirs, query, normed, latents, middle_grad, vectors, groups):
    rows, width = query.shape
    lanes = blocks[0].shape[-1]
    outs = term_shapes(groups, width // groups, lanes)
    result = pl.pallas_call(
        functools.partial(query_back_kernel, len(blocks), len(outs)),
        out_shape=[shape((rows // 2, width), single), shape((8, width), single)] + outs,
        in_specs=[scalars] + [remote] * len(blocks) + [whole] * 7,
        out_specs=[whole] * (2 + len(outs)),
        scratch_shapes=[
            pltpu.VMEM((2, width, lanes), half),
            pltpu.VMEM((rows, 2 * main), half),
            pltpu.VMEM((rows, width), half),
            pltpu.VMEM((rows // 2, width), single),
            pltpu.VMEM((width, lanes), single),
            pltpu.SemaphoreType.DMA((len(blocks),)),
        ],
        compiler_params=params,
        name="query_back",
    )(spot, *blocks, mine, theirs, query, normed, latents, middle_grad, vectors)
    return result[:2], result[2:]


def local(
    latents,
    pixels,
    keep_mask,
    cotangent,
    square_weights,
    square_first,
    square_second,
    pixel_weights,
    pixel_first,
    pixel_second,
    latent_vectors,
    latent_first,
    latent_second,
    pixel_norm,
    pixel_norm_first,
    pixel_norm_second,
):
    width = latents.shape[2]
    feats = pixels.shape[2]
    scale = width ** (-0.5)
    shard_width = square_weights.shape[2]
    rank = lax.axis_index("seq")
    groups = lax.axis_size("dp")
    part = width // 2
    spot = jnp.stack([lax.axis_index("dp"), rank]).astype(jnp.int32)

    def turned(array):
        return jnp.transpose(array, (0, 2, 1))

    square_p, square_m, square_v = turned(square_weights), turned(square_first), turned(square_second)
    pixel_p, pixel_m, pixel_v = turned(pixel_weights), turned(pixel_first), turned(pixel_second)
    square_copy = square_p.astype(half)
    pixel_copy = jnp.pad(pixel_p.astype(half), ((0, 0), (0, 0), (0, 2 * main - feats)))
    early_blocks = gather_matrices(square_copy[:1], pixel_copy[0])
    late_blocks = gather_matrices(square_copy[1:], pixel_copy[1])

    latents_two = (latents[0], trade(latents[0]))
    cotangent_two = (cotangent[0], trade(cotangent[0]))
    pixels_t = jnp.transpose(pixels, (2, 0, 1))
    gain, shift = pixel_norm[0][:, None], pixel_norm[1][:, None]
    pixel_normed, pixel_stats = norm_pixels(pixels_t, gain, shift)
    normed = norm_latents(*latents_two, latent_vectors)
    query, query_pix, sent = attend(spot, early_blocks, normed, pixel_normed, keep_mask, scale, feats)
    (latents_out, middle_grad, grad_pix, stats, chain_sums), early_terms = chain(
        spot, late_blocks, sent, trade(sent), latents_two, cotangent_two, latent_vectors, feats, groups
    )
    score_pix, pixels_grad, pixel_sums = pixel_back(
        query_pix, grad_pix, stats, pixel_normed, keep_mask, pixels_t, gain, pixel_stats, scale
    )
    (latents_grad, query_sums), late_terms = query_back(
        spot, early_blocks, score_pix, trade(score_pix), query, normed, latents[0], middle_grad, latent_vectors, groups
    )
    early = scatter_sum(early_terms, groups)
    late = scatter_sum(late_terms, groups)

    first = rank == 0

    def joined(array):
        other = trade(array)
        return jnp.where(first, array, other), jnp.where(first, other, array)

    early_low, early_high = joined(early)
    late_low, late_high = joined(late)

    def square(low, high, m):
        return jnp.concatenate([low[:, m * part : (m + 1) * part], high[:, m * part : (m + 1) * part]], axis=1)

    def pixel(low, high, m):
        return jnp.concatenate(
            [low[:, m * part : m * part + main], high[:, m * part : m * part + feats - main]], axis=1
        )

    square_grad = jnp.stack([square(late_low, late_high, 0)] + [square(early_low, early_high, m) for m in range(3)])
    pixel_weight_grad = jnp.stack([pixel(late_low, late_high, 1), pixel(early_low, early_high, 3)])

    norm_terms = jnp.pad(jnp.transpose(pixel_sums[:, :2]), ((6, 0), (0, width - feats)))
    vector_sums = sum_all(chain_sums + query_sums + norm_terms, True)
    latent_vector_grad, pixel_norm_grad = vector_sums[:6], vector_sums[6:, :feats]
    square_first_new, square_second_new, square_ratio = adam_moments(square_grad, square_m, square_v)
    pixel_first_new, pixel_second_new, pixel_ratio = adam_moments(pixel_weight_grad, pixel_m, pixel_v)
    square_update = square_ratio + decay_rate * square_p
    pixel_update = pixel_ratio + decay_rate * pixel_p
    weight_squares = jnp.concatenate(
        [jnp.sum(square_p * square_p, axis=(1, 2)), jnp.sum(pixel_p * pixel_p, axis=(1, 2))]
    )
    update_squares = jnp.concatenate(
        [jnp.sum(square_update * square_update, axis=(1, 2)), jnp.sum(pixel_update * pixel_update, axis=(1, 2))]
    )
    square_sums = sum_all(jnp.concatenate([weight_squares, update_squares]), False)
    weight_norm = jnp.sqrt(square_sums[:6])
    update_norm = jnp.sqrt(square_sums[6:])
    trust = weight_norm / (update_norm + epsilon)
    square_new = square_p - learn_rate * trust[:4, None, None] * square_update
    pixel_new = pixel_p - learn_rate * trust[4:, None, None] * pixel_update
    latent_first_new, latent_second_new, latent_ratio = adam_moments(latent_vector_grad, latent_first, latent_second)
    latent_vectors_new = latent_vectors - vector_rate * latent_ratio
    pixel_norm_first_new, pixel_norm_second_new, norm_ratio = adam_moments(
        pixel_norm_grad, pixel_norm_first, pixel_norm_second
    )
    pixel_norm_new = pixel_norm - vector_rate * norm_ratio
    matrix_norms = jnp.stack([weight_norm, update_norm, trust])
    return (
        latents_out[None],
        latents_grad[None],
        jnp.transpose(pixels_grad, (1, 2, 0)),
        turned(square_grad),
        turned(square_first_new),
        turned(square_second_new),
        turned(square_new),
        turned(square_new.astype(half)),
        turned(pixel_weight_grad),
        turned(pixel_first_new),
        turned(pixel_second_new),
        turned(pixel_new),
        turned(pixel_new.astype(half)),
        latent_first_new,
        latent_second_new,
        latent_vectors_new,
        pixel_norm_first_new,
        pixel_norm_second_new,
        pixel_norm_new,
        matrix_norms,
    )


def solution(mesh):
    return jax.shard_map(
        local,
        mesh=mesh,
        in_specs=(
            P("dp", "seq", None),
            P("dp", "seq", None),
            P("dp", "seq"),
            P("dp", "seq", None),
            P(None, None, "dp"),
            P(None, None, "dp"),
            P(None, None, "dp"),
            P(None, None, "dp"),
            P(None, None, "dp"),
            P(None, None, "dp"),
            P(),
            P(),
            P(),
            P(),
            P(),
            P(),
        ),
        out_specs=(
            P("dp", "seq", None),
            P("dp", "seq", None),
            P("dp", "seq", None),
            P(None, None, "dp"),
            P(None, None, "dp"),
            P(None, None, "dp"),
            P(None, None, "dp"),
            P(None, None, "dp"),
            P(None, None, "dp"),
            P(None, None, "dp"),
            P(None, None, "dp"),
            P(None, None, "dp"),
            P(None, None, "dp"),
            P(),
            P(),
            P(),
            P(),
            P(),
            P(),
            P(),
        ),
        check_vma=False,
    )
```

profile of v0, /device:TPU:0, one launch (start us, length us, event | category | flops | bytes accessed | tf_op | source)
XLA Modules:
  0.0 283.5 jit_solution(2772982541183690448)
XLA Ops:
  1.7 1.4 bitcast_convert_fusion
  3.2 4.1 %collective-permute-start.46 = (bf16[64,768]{1,0:T(8,128)(2,1)S(1)}, bf16[64,768]{1,0:T(8,128)(2,1)S(1)}, u32[]{:S(2)}, u32[]{:S(2)}) collective-permute-start(bf16[64,768]{1,0:T(8,128)(2,1)S(1)} %pad_maximum_fusion.5.refs_0_), channel_id=1, source_target_pairs={{0,16},{2,18},{4,20},{6,22},{8,24},{10,26},{12,28},{14,30},{16,0},... | collective-permute-start | bytes 294920 | tf_op jit(solution)/shard_map/ppermute | solution.py:65
  7.3 1.6 collective-permute-start.38
  8.9 1.5 collective-permute-start.34
  10.4 1.5 collective-permute-start.32
  13.0 1.5 collective-permute-start.50
  14.5 1.5 collective-permute-start.48
  19.1 2.2 collective-permute-start.36
  22.2 3.4 %collective-permute-start.15 = (bf16[64,1792]{1,0:T(8,128)(2,1)S(1)}, bf16[64,1792]{1,0:T(8,128)(2,1)S(1)}, u32[]{:S(2)}, u32[]{:S(2)}) collective-permute-start(bf16[64,1792]{1,0:T(8,128)(2,1)S(1)} %pad_maximum_fusion.3.refs_0_), channel_id=1, source_target_pairs={{0,16},{2,18},{4,20},{6,22},{8,24},{10,26},{12,28},{14,30},{16,0},... | collective-permute-start | bytes 688136 | tf_op jit(solution)/shard_map/ppermute | solution.py:65
  25.7 1.5 collective-permute-start.3
  27.2 2.4 collective-permute-start.1
  29.6 6.7 %collective-permute-done.15.refs_16_ = bf16[64,1792]{1,0:T(8,128)(2,1)S(1)} collective-permute-done((bf16[64,1792]{1,0:T(8,128)(2,1)S(1)}, bf16[64,1792]{1,0:T(8,128)(2,1)S(1)}, u32[]{:S(2)}, u32[]{:S(2)}) %collective-permute-start.15) | collective-permute-done | bytes 229408 | tf_op jit(solution)/shard_map/ppermute | solution.py:65
  37.6 1.8 collective-permute-start.52
  40.9 2.0 collective-permute-done.56.refs_26_
  46.4 2.1 collective-permute-done.44.refs_14_
  50.8 3.4 %collective-permute-done.60.refs_30_ = bf16[64,768]{1,0:T(8,128)(2,1)S(1)} collective-permute-done((bf16[64,768]{1,0:T(8,128)(2,1)S(1)}, bf16[64,768]{1,0:T(8,128)(2,1)S(1)}, u32[]{:S(2)}, u32[]{:S(2)}) %collective-permute-start.60) | collective-permute-done | bytes 98336 | tf_op jit(solution)/shard_map/ppermute | solution.py:65
  57.3 1.5 collective-permute-done.19.refs_20_
  59.5 4.6 %collective-permute-done.17.refs_18_ = bf16[64,1792]{1,0:T(8,128)(2,1)} collective-permute-done((bf16[64,1792]{1,0:T(8,128)(2,1)S(1)}, bf16[64,1792]{1,0:T(8,128)(2,1)}, u32[]{:S(2)}, u32[]{:S(2)}) %collective-permute-start.17) | collective-permute-done | bytes 229408 | tf_op jit(solution)/shard_map/ppermute | solution.py:65
  65.0 3.9 %collective-permute-done.9.refs_10_ = bf16[64,1792]{1,0:T(8,128)(2,1)S(1)} collective-permute-done((bf16[64,1792]{1,0:T(8,128)(2,1)S(1)}, bf16[64,1792]{1,0:T(8,128)(2,1)S(1)}, u32[]{:S(2)}, u32[]{:S(2)}) %collective-permute-start.9) | collective-permute-done | bytes 229408 | tf_op jit(solution)/shard_map/ppermute | solution.py:65
  69.9 3.1 %collective-permute-done.5.refs_6_ = bf16[64,1792]{1,0:T(8,128)(2,1)S(1)} collective-permute-done((bf16[64,1792]{1,0:T(8,128)(2,1)S(1)}, bf16[64,1792]{1,0:T(8,128)(2,1)S(1)}, u32[]{:S(2)}, u32[]{:S(2)}) %collective-permute-start.5) | collective-permute-done | bytes 229408 | tf_op jit(solution)/shard_map/ppermute | solution.py:65
  77.6 2.6 collective-permute-done.25.refs_26_
  83.1 7.5 %norm_pixels.1 = (bf16[384,4096]{1,0:T(8,128)(2,1)}, f32[2,4096]{1,0:T(2,128)}) custom-call(f32[261,1,4096]{2,1,0:T(1,128)} %bitcast.191, f32[261,1]{1,0:T(8,128)} %copy.43.gain, f32[261,1]{1,0:T(8,128)} %copy.44.shift), custom_call_target="tpu_custom_call" | custom-call | tf_op jit(solution)/shard_map/norm_pixels/pallas_call | solution.py:231
  91.2 3.1 %norm_latents.1.refs_32_.refs_35_ = bf16[512,1024]{1,0:T(8,128)(2,1)} custom-call(f32[256,1024]{1,0:T(8,128)} %bitcast.193, f32[256,1024]{1,0:T(8,128)} %copy-done.2, f32[6,1024]{1,0:T(8,128)} %refs_38_.3), custom_call_target="tpu_custom_call" | custom-call | tf_op jit(solution)/shard_map/norm_latents/pallas_call | solution.py:250
  94.4 15.4 %attend.1 = (bf16[512,1024]{1,0:T(8,128)(2,1)}, bf16[512,384]{1,0:T(8,128)(2,1)}, f32[512,384]{1,0:T(8,128)}) custom-call(s32[2]{0:T(128)} %pad_add_fusion.1.spot, bf16[64,768]{1,0:T(8,128)(2,1)} %copy-done.10, bf16[64,768]{1,0:T(8,128)(2,1)} %copy-done.20, bf16[64,768]{1,0:T(8,128)(2,1)} %copy-done.19, bf16[64,768]{1,0:T(8,128)(2,1)} %copy-done.30, ...), custom_call_target="tpu_custom_call" | custom-call | tf_op jit(solution)/shard_map/attend/pallas_call | solution.py:298
  111.6 6.3 %collective-permute-done.13.refs_14_ = bf16[64,1792]{1,0:T(8,128)(2,1)S(1)} collective-permute-done((bf16[64,1792]{1,0:T(8,128)(2,1)S(1)}, bf16[64,1792]{1,0:T(8,128)(2,1)S(1)}, u32[]{:S(2)}, u32[]{:S(2)}) %collective-permute-start.13) | collective-permute-done | bytes 229408 | tf_op jit(solution)/shard_map/ppermute | solution.py:65
  119.5 6.5 %collective-permute-done.29.refs_30_ = bf16[64,1792]{1,0:T(8,128)(2,1)S(1)} collective-permute-done((bf16[64,1792]{1,0:T(8,128)(2,1)S(1)}, bf16[64,1792]{1,0:T(8,128)(2,1)S(1)}, u32[]{:S(2)}, u32[]{:S(2)}) %collective-permute-start.29) | collective-permute-done | bytes 229408 | tf_op jit(solution)/shard_map/ppermute | solution.py:65
  129.4 20.0 %chain.1 = (f32[256,1024]{1,0:T(8,128)}, f32[256,1024]{1,0:T(8,128)}, bf16[512,384]{1,0:T(8,128)(2,1)}, f32[512,128]{1,0:T(8,128)}, f32[8,1024]{1,0:T(8,128)}, /...) custom-call(s32[2]{0:T(128)} %pad_add_fusion.1.spot, ...), custom_call_target="tpu_custom_call" | custom-call | tf_op jit(solution)/shard_map/chain/pallas_call | solution.py:402
  149.3 19.0 %pixel_back.1 = (f32[512,384]{1,0:T(8,128)}, f32[261,1,4096]{2,1,0:T(1,128)}, f32[261,128]{1,0:T(8,128)}) custom-call(bf16[512,384]{1,0:T(8,128)(2,1)} %get-tuple-element.46.query_pix, bf16[512,384]{1,0:T(8,128)(2,1)} %get-tuple-element.47.grad_pix, f32[512,128]{1,0:T(8,128)} %get-tuple-element.48.stats, ...), custom_call_target="tpu_custom_call" | custom-call | tf_op jit(solution)/shard_map/pixel_back/pallas_call | solution.py:491
  171.9 8.7 %query_back.1 = (f32[256,1024]{1,0:T(8,128)}, f32[8,1024]{1,0:T(8,128)}, bf16[8,32,768]{2,1,0:T(8,128)(2,1)}, bf16[8,32,768]{2,1,0:T(8,128)(2,1)}, bf16[8,32,768...) custom-call(s32[2]{0:T(128)} %pad_add_fusion.1.spot, bf16[64,768]{1,0:T(8,128)(2,1)} %copy-done.10, ...), custom_call_target="tpu_custom_call" | custom-call | tf_op jit(solution)/shard_map/query_back/pallas_call | solution.py:552
  189.0 1.9 collective-permute-start.92
  191.2 2.3 collective-permute-start.90
  198.4 11.2 %collective-permute-done.73 = bf16[8,32,1792]{2,1,0:T(8,128)(2,1)S(1)} collective-permute-done((bf16[8,32,1792]{2,1,0:T(8,128)(2,1)}, bf16[8,32,1792]{2,1,0:T(8,128)(2,1)S(1)}, u32[]{:S(2)}, u32[]{:S(2)}) %collective-permute-start.73) | collective-permute-done | bytes 917536 | tf_op jit(solution)/shard_map/ppermute | solution.py:65
  210.9 5.9 %collective-permute-done.75 = bf16[8,32,1792]{2,1,0:T(8,128)(2,1)S(1)} collective-permute-done((bf16[8,32,1792]{2,1,0:T(8,128)(2,1)S(1)}, bf16[8,32,1792]{2,1,0:T(8,128)(2,1)S(1)}, u32[]{:S(2)}, u32[]{:S(2)}) %collective-permute-start.75) | collective-permute-done | bytes 917536 | tf_op jit(solution)/shard_map/ppermute | solution.py:65
  217.1 1.3 collective-permute-start.76
  219.6 5.7 %collective-permute-done.68 = bf16[8,32,768]{2,1,0:T(8,128)(2,1)S(1)} collective-permute-done((bf16[8,32,768]{2,1,0:T(8,128)(2,1)}, bf16[8,32,768]{2,1,0:T(8,128)(2,1)S(1)}, u32[]{:S(2)}, u32[]{:S(2)}) %collective-permute-start.68) | collective-permute-done | bytes 393248 | tf_op jit(solution)/shard_map/ppermute | solution.py:65
  226.7 9.2 %collective-permute-done.67 = bf16[4,32,768]{2,1,0:T(8,128)(2,1)S(1)} collective-permute-done((bf16[4,32,768]{2,1,0:T(8,128)(2,1)S(1)}, bf16[4,32,768]{2,1,0:T(8,128)(2,1)S(1)}, u32[]{:S(2)}, u32[]{:S(2)}) %collective-permute-start.67) | collective-permute-done | bytes 196640 | tf_op jit(solution)/shard_map/ppermute | solution.py:65
  236.8 1.8 collective-permute-start.77
  238.6 6.4 %collective-permute-done.70 = bf16[2,64,768]{2,1,0:T(8,128)(2,1)S(1)} collective-permute-done((bf16[2,64,768]{2,1,0:T(8,128)(2,1)S(1)}, bf16[2,64,768]{2,1,0:T(8,128)(2,1)S(1)}, u32[]{:S(2)}, u32[]{:S(2)}) %collective-permute-start.70) | collective-permute-done | bytes 196640 | tf_op jit(solution)/shard_map/ppermute | solution.py:65
  245.2 6.3 %collective-permute-done.77 = bf16[2,64,1792]{2,1,0:T(8,128)(2,1)S(1)} collective-permute-done((bf16[2,64,1792]{2,1,0:T(8,128)(2,1)S(1)}, bf16[2,64,1792]{2,1,0:T(8,128)(2,1)S(1)}, u32[]{:S(2)}, u32[]{:S(2)}) %collective-permute-start.77) | collective-permute-done | bytes 458784 | tf_op jit(solution)/shard_map/ppermute | solution.py:65
  251.6 1.8 collective-permute-start.78
  253.4 1.6 collective-permute-done.71
  255.1 6.4 %collective-permute-done.78 = bf16[1,64,1792]{2,1,0:T(8,128)(2,1)S(1)} collective-permute-done((bf16[1,64,1792]{2,1,0:T(8,128)(2,1)S(1)}, bf16[1,64,1792]{2,1,0:T(8,128)(2,1)S(1)}, u32[]{:S(2)}, u32[]{:S(2)}) %collective-permute-start.78) | collective-permute-done | bytes 229408 | tf_op jit(solution)/shard_map/ppermute | solution.py:65
  261.8 1.6 collective-permute-done.79
  265.7 2.5 multiply_reduce_fusion
  268.3 1.7 collective-permute-start.82
  274.6 1.4 collective-permute-start.85
  276.0 2.9 %collective-permute-start.83 = (f32[12]{0:T(128)S(1)}, f32[12]{0:T(128)S(1)}, u32[]{:S(2)}, u32[]{:S(2)}) collective-permute-start(f32[12]{0:T(128)S(1)} %add_add_fusion.3), channel_id=1, source_target_pairs={{0,8},{2,10},{4,12},{6,14},{8,0},{10,2},{12,4},{14,6},{16,24},{18,... | collective-permute-start | bytes 152 | tf_op jit(solution)/shard_map/ppermute | solution.py:65
  281.5 1.4 convert_bitcast_fusion
  (386 shorter events, 67.1 us)
Async XLA Ops:
  3.2 8.9 %collective-permute-start.46 = (bf16[64,768]{1,0:T(8,128)(2,1)S(1)}, bf16[64,768]{1,0:T(8,128)(2,1)S(1)}, u32[]{:S(2)}, u32[]{:S(2)}) collective-permute-start(bf16[64,768]{1,0:T(8,128)(2,1)S(1)} %pad_maximum_fusion.5.refs_0_), channel_id=1, source_target_pairs={{0,16},{2,18},{4,20},{6,22},{8,24},{10,26},{12,28},{14,30},{16,0},... | collective-permute-start | bytes 294920 | tf_op jit(solution)/shard_map/ppermute | solution.py:65
  18.5 7.1 %collective-permute-start.39 = (bf16[64,768]{1,0:T(8,128)(2,1)S(1)}, bf16[64,768]{1,0:T(8,128)(2,1)S(1)}, u32[]{:S(2)}, u32[]{:S(2)}) collective-permute-start(bf16[64,768]{1,0:T(8,128)(2,1)S(1)} %collective-permute-done.38.refs_8_), channel_id=1, source_target_pairs={{0,1},{1,0},{2,3},{3,2},{4,5},{5,4},{6,7},{7,6},{8,9},{9,8},{10,11... | collective-permute-start | bytes 294920 | tf_op jit(solution)/shard_map/ppermute | solution.py:69
  19.1 6.6 %collective-permute-start.36 = (bf16[64,768]{1,0:T(8,128)(2,1)S(1)}, bf16[64,768]{1,0:T(8,128)(2,1)S(1)}, u32[]{:S(2)}, u32[]{:S(2)}) collective-permute-start(bf16[64,768]{1,0:T(8,128)(2,1)S(1)} %collective-permute-done.34.refs_4_), channel_id=1, source_target_pairs={{0,2},{2,0},{4,6},{6,4},{8,10},{10,8},{12,14},{14,12},{16,18},{18,... | collective-permute-start | bytes 294920 | tf_op jit(solution)/shard_map/ppermute | solution.py:65
  21.3 5.9 %collective-permute-start.35 = (bf16[64,768]{1,0:T(8,128)(2,1)S(1)}, bf16[64,768]{1,0:T(8,128)(2,1)S(1)}, u32[]{:S(2)}, u32[]{:S(2)}) collective-permute-start(bf16[64,768]{1,0:T(8,128)(2,1)S(1)} %collective-permute-done.34.refs_4_), channel_id=1, source_target_pairs={{0,1},{1,0},{2,3},{3,2},{4,5},{5,4},{6,7},{7,6},{8,9},{9,8},{10,11... | collective-permute-start | bytes 294920 | tf_op jit(solution)/shard_map/ppermute | solution.py:69
  21.4 8.2 %collective-permute-start.33 = (bf16[64,768]{1,0:T(8,128)(2,1)S(1)}, bf16[64,768]{1,0:T(8,128)(2,1)S(1)}, u32[]{:S(2)}, u32[]{:S(2)}) collective-permute-start(bf16[64,768]{1,0:T(8,128)(2,1)S(1)} %collective-permute-done.32.refs_2_), channel_id=1, source_target_pairs={{0,1},{1,0},{2,3},{3,2},{4,5},{5,4},{6,7},{7,6},{8,9},{9,8},{10,11... | collective-permute-start | bytes 294920 | tf_op jit(solution)/shard_map/ppermute | solution.py:69
  22.2 14.1 %collective-permute-start.15 = (bf16[64,1792]{1,0:T(8,128)(2,1)S(1)}, bf16[64,1792]{1,0:T(8,128)(2,1)S(1)}, u32[]{:S(2)}, u32[]{:S(2)}) collective-permute-start(bf16[64,1792]{1,0:T(8,128)(2,1)S(1)} %pad_maximum_fusion.3.refs_0_), channel_id=1, source_target_pairs={{0,16},{2,18},{4,20},{6,22},{8,24},{10,26},{12,28},{14,30},{16,0},... | collective-permute-start | bytes 688136 | tf_op jit(solution)/shard_map/ppermute | solution.py:65
  25.6 11.7 %collective-permute-start.7 = (bf16[64,1792]{1,0:T(8,128)(2,1)S(1)}, bf16[64,1792]{1,0:T(8,128)(2,1)S(1)}, u32[]{:S(2)}, u32[]{:S(2)}) collective-permute-start(bf16[64,1792]{1,0:T(8,128)(2,1)S(1)} %pad_maximum_fusion.3.refs_0_), channel_id=1, source_target_pairs={{0,8},{2,10},{4,12},{6,14},{8,0},{10,2},{12,4},{14,6},{16,24},{18,... | collective-permute-start | bytes 688136 | tf_op jit(solution)/shard_map/ppermute | solution.py:65
  25.7 11.9 %collective-permute-start.3 = (bf16[64,1792]{1,0:T(8,128)(2,1)S(1)}, bf16[64,1792]{1,0:T(8,128)(2,1)S(1)}, u32[]{:S(2)}, u32[]{:S(2)}) collective-permute-start(bf16[64,1792]{1,0:T(8,128)(2,1)S(1)} %pad_maximum_fusion.3.refs_0_), channel_id=1, source_target_pairs={{0,4},{2,6},{4,0},{6,2},{8,12},{10,14},{12,8},{14,10},{16,20},{18,... | collective-permute-start | bytes 688136 | tf_op jit(solution)/shard_map/ppermute | solution.py:65
  27.2 10.4 %collective-permute-start.1 = (bf16[64,1792]{1,0:T(8,128)(2,1)S(1)}, bf16[64,1792]{1,0:T(8,128)(2,1)S(1)}, u32[]{:S(2)}, u32[]{:S(2)}) collective-permute-start(bf16[64,1792]{1,0:T(8,128)(2,1)S(1)} %pad_maximum_fusion.3.refs_0_), channel_id=1, source_target_pairs={{0,2},{2,0},{4,6},{6,4},{8,10},{10,8},{12,14},{14,12},{16,18},{18,... | collective-permute-start | bytes 688136 | tf_op jit(solution)/shard_map/ppermute | solution.py:65
  29.6 9.9 %collective-permute-start = (bf16[64,1792]{1,0:T(8,128)(2,1)S(1)}, bf16[64,1792]{1,0:T(8,128)(2,1)S(1)}, u32[]{:S(2)}, u32[]{:S(2)}) collective-permute-start(bf16[64,1792]{1,0:T(8,128)(2,1)S(1)} %pad_maximum_fusion.3.refs_0_), channel_id=1, source_target_pairs={{0,1},{1,0},{2,3},{3,2},{4,5},{5,4},{6,7},{7,6},{8,9},{9,8},{10,11... | collective-permute-start | bytes 688136 | tf_op jit(solution)/shard_map/ppermute | solution.py:69
  37.6 6.3 %collective-permute-start.52 = (bf16[64,768]{1,0:T(8,128)(2,1)S(1)}, bf16[64,768]{1,0:T(8,128)(2,1)S(1)}, u32[]{:S(2)}, u32[]{:S(2)}) collective-permute-start(bf16[64,768]{1,0:T(8,128)(2,1)S(1)} %collective-permute-done.50.refs_20_), channel_id=1, source_target_pairs={{0,2},{2,0},{4,6},{6,4},{8,10},{10,8},{12,14},{14,12},{16,18},{18,... | collective-permute-start | bytes 294920 | tf_op jit(solution)/shard_map/ppermute | solution.py:65
  42.9 37.8 %collective-permute-start.62 = (f32[256,1024]{1,0:T(8,128)S(1)}, f32[256,1024]{1,0:T(8,128)S(1)}, u32[]{:S(2)}, u32[]{:S(2)}) collective-permute-start(f32[256,1024]{1,0:T(8,128)S(1)} %bitcast.196), channel_id=1, source_target_pairs={{0,1},{1,0},{2,3},{3,2},{4,5},{5,4},{6,7},{7,6},{8,9},{9,8},{10,11... | collective-permute-start | bytes 3145736 | tf_op jit(solution)/shard_map/ppermute | solution.py:69
  45.8 10.4 %collective-permute-start.23 = (bf16[64,1792]{1,0:T(8,128)(2,1)S(1)}, bf16[64,1792]{1,0:T(8,128)(2,1)S(1)}, u32[]{:S(2)}, u32[]{:S(2)}) collective-permute-start(bf16[64,1792]{1,0:T(8,128)(2,1)S(1)} %collective-permute-done.15.refs_16_), channel_id=1, source_target_pairs={{0,8},{2,10},{4,12},{6,14},{8,0},{10,2},{12,4},{14,6},{16,24},{18,... | collective-permute-start | bytes 688136 | tf_op jit(solution)/shard_map/ppermute | solution.py:65
  49.8 8.9 %collective-permute-start.19 = (bf16[64,1792]{1,0:T(8,128)(2,1)S(1)}, bf16[64,1792]{1,0:T(8,128)(2,1)}, u32[]{:S(2)}, u32[]{:S(2)}) collective-permute-start(bf16[64,1792]{1,0:T(8,128)(2,1)S(1)} %collective-permute-done.15.refs_16_), channel_id=1, source_target_pairs={{0,4},{2,6},{4,0},{6,2},{8,12},{10,14},{12,8},{14,10},{16,20},{18,... | collective-permute-start | bytes 688136 | tf_op jit(solution)/shard_map/ppermute | solution.py:65
  55.5 8.6 %collective-permute-start.17 = (bf16[64,1792]{1,0:T(8,128)(2,1)S(1)}, bf16[64,1792]{1,0:T(8,128)(2,1)}, u32[]{:S(2)}, u32[]{:S(2)}) collective-permute-start(bf16[64,1792]{1,0:T(8,128)(2,1)S(1)} %collective-permute-done.15.refs_16_), channel_id=1, source_target_pairs={{0,2},{2,0},{4,6},{6,4},{8,10},{10,8},{12,14},{14,12},{16,18},{18,... | collective-permute-start | bytes 688136 | tf_op jit(solution)/shard_map/ppermute | solution.py:65
  56.2 7.9 %collective-permute-start.16 = (bf16[64,1792]{1,0:T(8,128)(2,1)S(1)}, bf16[64,1792]{1,0:T(8,128)(2,1)S(1)}, u32[]{:S(2)}, u32[]{:S(2)}) collective-permute-start(bf16[64,1792]{1,0:T(8,128)(2,1)S(1)} %collective-permute-done.15.refs_16_), channel_id=1, source_target_pairs={{0,1},{1,0},{2,3},{3,2},{4,5},{5,4},{6,7},{7,6},{8,9},{9,8},{10,11... | collective-permute-start | bytes 688136 | tf_op jit(solution)/shard_map/ppermute | solution.py:69
  56.2 8.6 %collective-permute-start.11 = (bf16[64,1792]{1,0:T(8,128)(2,1)S(1)}, bf16[64,1792]{1,0:T(8,128)(2,1)}, u32[]{:S(2)}, u32[]{:S(2)}) collective-permute-start(bf16[64,1792]{1,0:T(8,128)(2,1)S(1)} %collective-permute-done.7.refs_8_), channel_id=1, source_target_pairs={{0,4},{2,6},{4,0},{6,2},{8,12},{10,14},{12,8},{14,10},{16,20},{18,... | collective-permute-start | bytes 688136 | tf_op jit(solution)/shard_map/ppermute | solution.py:65
  58.8 10.1 %collective-permute-start.9 = (bf16[64,1792]{1,0:T(8,128)(2,1)S(1)}, bf16[64,1792]{1,0:T(8,128)(2,1)S(1)}, u32[]{:S(2)}, u32[]{:S(2)}) collective-permute-start(bf16[64,1792]{1,0:T(8,128)(2,1)S(1)} %collective-permute-done.7.refs_8_), channel_id=1, source_target_pairs={{0,2},{2,0},{4,6},{6,4},{8,10},{10,8},{12,14},{14,12},{16,18},{18,... | collective-permute-start | bytes 688136 | tf_op jit(solution)/shard_map/ppermute | solution.py:65
  64.1 8.9 %collective-permute-start.5 = (bf16[64,1792]{1,0:T(8,128)(2,1)S(1)}, bf16[64,1792]{1,0:T(8,128)(2,1)S(1)}, u32[]{:S(2)}, u32[]{:S(2)}) collective-permute-start(bf16[64,1792]{1,0:T(8,128)(2,1)S(1)} %collective-permute-done.3.refs_4_), channel_id=1, source_target_pairs={{0,2},{2,0},{4,6},{6,4},{8,10},{10,8},{12,14},{14,12},{16,18},{18,... | collective-permute-start | bytes 688136 | tf_op jit(solution)/shard_map/ppermute | solution.py:65
  64.8 8.9 %collective-permute-start.4 = (bf16[64,1792]{1,0:T(8,128)(2,1)S(1)}, bf16[64,1792]{1,0:T(8,128)(2,1)S(1)}, u32[]{:S(2)}, u32[]{:S(2)}) collective-permute-start(bf16[64,1792]{1,0:T(8,128)(2,1)S(1)} %collective-permute-done.3.refs_4_), channel_id=1, source_target_pairs={{0,1},{1,0},{2,3},{3,2},{4,5},{5,4},{6,7},{7,6},{8,9},{9,8},{10,11... | collective-permute-start | bytes 688136 | tf_op jit(solution)/shard_map/ppermute | solution.py:69
  68.9 8.0 %collective-permute-start.27 = (bf16[64,1792]{1,0:T(8,128)(2,1)S(1)}, bf16[64,1792]{1,0:T(8,128)(2,1)S(1)}, u32[]{:S(2)}, u32[]{:S(2)}) collective-permute-start(bf16[64,1792]{1,0:T(8,128)(2,1)S(1)} %collective-permute-done.23.refs_24_), channel_id=1, source_target_pairs={{0,4},{2,6},{4,0},{6,2},{8,12},{10,14},{12,8},{14,10},{16,20},{18,... | collective-permute-start | bytes 688136 | tf_op jit(solution)/shard_map/ppermute | solution.py:65
  73.0 7.2 %collective-permute-start.25 = (bf16[64,1792]{1,0:T(8,128)(2,1)S(1)}, bf16[64,1792]{1,0:T(8,128)(2,1)S(1)}, u32[]{:S(2)}, u32[]{:S(2)}) collective-permute-start(bf16[64,1792]{1,0:T(8,128)(2,1)S(1)} %collective-permute-done.23.refs_24_), channel_id=1, source_target_pairs={{0,2},{2,0},{4,6},{6,4},{8,10},{10,8},{12,14},{14,12},{16,18},{18,... | collective-permute-start | bytes 688136 | tf_op jit(solution)/shard_map/ppermute | solution.py:65
  73.7 6.5 %collective-permute-start.24 = (bf16[64,1792]{1,0:T(8,128)(2,1)S(1)}, bf16[64,1792]{1,0:T(8,128)(2,1)S(1)}, u32[]{:S(2)}, u32[]{:S(2)}) collective-permute-start(bf16[64,1792]{1,0:T(8,128)(2,1)S(1)} %collective-permute-done.23.refs_24_), channel_id=1, source_target_pairs={{0,1},{1,0},{2,3},{3,2},{4,5},{5,4},{6,7},{7,6},{8,9},{9,8},{10,11... | collective-permute-start | bytes 688136 | tf_op jit(solution)/shard_map/ppermute | solution.py:69
  75.3 52.1 %collective-permute-start.64 = (f32[256,1024]{1,0:T(8,128)S(1)}, f32[256,1024]{1,0:T(8,128)}, u32[]{:S(2)}, u32[]{:S(2)}) collective-permute-start(f32[256,1024]{1,0:T(8,128)S(1)} %bitcast.210), channel_id=1, source_target_pairs={{0,1},{1,0},{2,3},{3,2},{4,5},{5,4},{6,7},{7,6},{8,9},{9,8},{10,11... | collective-permute-start | bytes 3145736 | tf_op jit(solution)/shard_map/ppermute | solution.py:69
  76.9 32.9 %collective-permute-start.21 = (bf16[64,1792]{1,0:T(8,128)(2,1)}, bf16[64,1792]{1,0:T(8,128)(2,1)}, u32[]{:S(2)}, u32[]{:S(2)}) collective-permute-start(bf16[64,1792]{1,0:T(8,128)(2,1)} %collective-permute-done.19.refs_20_), channel_id=1, source_target_pairs={{0,2},{2,0},{4,6},{6,4},{8,10},{10,8},{12,14},{14,12},{16,18},{18,... | collective-permute-start | bytes 688136 | tf_op jit(solution)/shard_map/ppermute | solution.py:65
  80.2 29.8 %collective-permute-start.20 = (bf16[64,1792]{1,0:T(8,128)(2,1)}, bf16[64,1792]{1,0:T(8,128)(2,1)}, u32[]{:S(2)}, u32[]{:S(2)}) collective-permute-start(bf16[64,1792]{1,0:T(8,128)(2,1)} %collective-permute-done.19.refs_20_), channel_id=1, source_target_pairs={{0,1},{1,0},{2,3},{3,2},{4,5},{5,4},{6,7},{7,6},{8,9},{9,8},{10,11... | collective-permute-start | bytes 688136 | tf_op jit(solution)/shard_map/ppermute | solution.py:69
  80.2 30.8 %collective-permute-start.18 = (bf16[64,1792]{1,0:T(8,128)(2,1)}, bf16[64,1792]{1,0:T(8,128)(2,1)}, u32[]{:S(2)}, u32[]{:S(2)}) collective-permute-start(bf16[64,1792]{1,0:T(8,128)(2,1)} %collective-permute-done.17.refs_18_), channel_id=1, source_target_pairs={{0,1},{1,0},{2,3},{3,2},{4,5},{5,4},{6,7},{7,6},{8,9},{9,8},{10,11... | collective-permute-start | bytes 688136 | tf_op jit(solution)/shard_map/ppermute | solution.py:69
  81.0 30.0 %collective-permute-start.12 = (bf16[64,1792]{1,0:T(8,128)(2,1)}, bf16[64,1792]{1,0:T(8,128)(2,1)S(1)}, u32[]{:S(2)}, u32[]{:S(2)}) collective-permute-start(bf16[64,1792]{1,0:T(8,128)(2,1)} %collective-permute-done.11.refs_12_), channel_id=1, source_target_pairs={{0,1},{1,0},{2,3},{3,2},{4,5},{5,4},{6,7},{7,6},{8,9},{9,8},{10,11... | collective-permute-start | bytes 688136 | tf_op jit(solution)/shard_map/ppermute | solution.py:69
  109.8 18.0 %collective-permute-start.63 = (f32[512,384]{1,0:T(8,128)}, f32[512,384]{1,0:T(8,128)S(1)}, u32[]{:S(2)}, u32[]{:S(2)}) collective-permute-start(f32[512,384]{1,0:T(8,128)} %get-tuple-element.44.refs_32_), channel_id=1, source_target_pairs={{0,1},{1,0},{2,3},{3,2},{4,5},{5,4},{6,7},{7,6},{8,9},{9,8},{10,11... | collective-permute-start | bytes 2359304 | tf_op jit(solution)/shard_map/ppermute | solution.py:69
  110.1 7.8 %collective-permute-start.13 = (bf16[64,1792]{1,0:T(8,128)(2,1)S(1)}, bf16[64,1792]{1,0:T(8,128)(2,1)S(1)}, u32[]{:S(2)}, u32[]{:S(2)}) collective-permute-start(bf16[64,1792]{1,0:T(8,128)(2,1)S(1)} %copy-done.55), channel_id=1, source_target_pairs={{0,4},{2,6},{4,0},{6,2},{8,12},{10,14},{12,8},{14,10},{16,20},{18,... | collective-permute-start | bytes 688136 | tf_op jit(solution)/shard_map/ppermute | solution.py:65
  111.0 6.9 %collective-permute-start.10 = (bf16[64,1792]{1,0:T(8,128)(2,1)S(1)}, bf16[64,1792]{1,0:T(8,128)(2,1)S(1)}, u32[]{:S(2)}, u32[]{:S(2)}) collective-permute-start(bf16[64,1792]{1,0:T(8,128)(2,1)S(1)} %copy-done.55), channel_id=1, source_target_pairs={{0,1},{1,0},{2,3},{3,2},{4,5},{5,4},{6,7},{7,6},{8,9},{9,8},{10,11... | collective-permute-start | bytes 688136 | tf_op jit(solution)/shard_map/ppermute | solution.py:69
  111.1 7.9 %collective-permute-start.6 = (bf16[64,1792]{1,0:T(8,128)(2,1)S(1)}, bf16[64,1792]{1,0:T(8,128)(2,1)S(1)}, u32[]{:S(2)}, u32[]{:S(2)}) collective-permute-start(bf16[64,1792]{1,0:T(8,128)(2,1)S(1)} %copy-done.58), channel_id=1, source_target_pairs={{0,1},{1,0},{2,3},{3,2},{4,5},{5,4},{6,7},{7,6},{8,9},{9,8},{10,11... | collective-permute-start | bytes 688136 | tf_op jit(solution)/shard_map/ppermute | solution.py:69
  117.9 8.1 %collective-permute-start.29 = (bf16[64,1792]{1,0:T(8,128)(2,1)S(1)}, bf16[64,1792]{1,0:T(8,128)(2,1)S(1)}, u32[]{:S(2)}, u32[]{:S(2)}) collective-permute-start(bf16[64,1792]{1,0:T(8,128)(2,1)S(1)} %copy-done.64), channel_id=1, source_target_pairs={{0,4},{2,6},{4,0},{6,2},{8,12},{10,14},{12,8},{14,10},{16,20},{18,... | collective-permute-start | bytes 688136 | tf_op jit(solution)/shard_map/ppermute | solution.py:65
  119.0 7.0 %collective-permute-start.26 = (bf16[64,1792]{1,0:T(8,128)(2,1)S(1)}, bf16[64,1792]{1,0:T(8,128)(2,1)S(1)}, u32[]{:S(2)}, u32[]{:S(2)}) collective-permute-start(bf16[64,1792]{1,0:T(8,128)(2,1)S(1)} %copy-done.64), channel_id=1, source_target_pairs={{0,1},{1,0},{2,3},{3,2},{4,5},{5,4},{6,7},{7,6},{8,9},{9,8},{10,11... | collective-permute-start | bytes 688136 | tf_op jit(solution)/shard_map/ppermute | solution.py:69
  119.4 7.1 %collective-permute-start.22 = (bf16[64,1792]{1,0:T(8,128)(2,1)}, bf16[64,1792]{1,0:T(8,128)(2,1)S(1)}, u32[]{:S(2)}, u32[]{:S(2)}) collective-permute-start(bf16[64,1792]{1,0:T(8,128)(2,1)} %collective-permute-done.21.refs_22_), channel_id=1, source_target_pairs={{0,1},{1,0},{2,3},{3,2},{4,5},{5,4},{6,7},{7,6},{8,9},{9,8},{10,11... | collective-permute-start | bytes 688136 | tf_op jit(solution)/shard_map/ppermute | solution.py:69
  186.1 23.5 %collective-permute-start.73 = (bf16[8,32,1792]{2,1,0:T(8,128)(2,1)}, bf16[8,32,1792]{2,1,0:T(8,128)(2,1)S(1)}, u32[]{:S(2)}, u32[]{:S(2)}) collective-permute-start(bf16[8,32,1792]{2,1,0:T(8,128)(2,1)} %get-tuple-element.60), channel_id=1, source_target_pairs={{0,2},{2,0},{4,6},{6,4},{8,10},{10,8},{12,14},{14,12},{16,18},{18,... | collective-permute-start | bytes 2752520 | tf_op jit(solution)/shard_map/ppermute | solution.py:65
  193.5 23.3 %collective-permute-start.75 = (bf16[8,32,1792]{2,1,0:T(8,128)(2,1)S(1)}, bf16[8,32,1792]{2,1,0:T(8,128)(2,1)S(1)}, u32[]{:S(2)}, u32[]{:S(2)}) collective-permute-start(bf16[8,32,1792]{2,1,0:T(8,128)(2,1)S(1)} %copy-done.84), channel_id=1, source_target_pairs={{0,4},{2,6},{4,0},{6,2},{8,12},{10,14},{12,8},{14,10},{16,20},{18,... | collective-permute-start | bytes 2752520 | tf_op jit(solution)/shard_map/ppermute | solution.py:65
  194.8 23.6 %collective-permute-start.66 = (bf16[8,32,768]{2,1,0:T(8,128)(2,1)}, bf16[8,32,768]{2,1,0:T(8,128)(2,1)S(1)}, u32[]{:S(2)}, u32[]{:S(2)}) collective-permute-start(bf16[8,32,768]{2,1,0:T(8,128)(2,1)} %get-tuple-element.56), channel_id=1, source_target_pairs={{0,2},{2,0},{4,6},{6,4},{8,10},{10,8},{12,14},{14,12},{16,18},{18,... | collective-permute-start | bytes 1179656 | tf_op jit(solution)/shard_map/ppermute | solution.py:65
  196.1 29.1 %collective-permute-start.68 = (bf16[8,32,768]{2,1,0:T(8,128)(2,1)}, bf16[8,32,768]{2,1,0:T(8,128)(2,1)S(1)}, u32[]{:S(2)}, u32[]{:S(2)}) collective-permute-start(bf16[8,32,768]{2,1,0:T(8,128)(2,1)} %get-tuple-element.58), channel_id=1, source_target_pairs={{0,4},{2,6},{4,0},{6,2},{8,12},{10,14},{12,8},{14,10},{16,20},{18,... | collective-permute-start | bytes 1179656 | tf_op jit(solution)/shard_map/ppermute | solution.py:65
  209.9 26.6 %collective-permute-start.74 = (bf16[4,32,1792]{2,1,0:T(8,128)(2,1)S(1)}, bf16[4,32,1792]{2,1,0:T(8,128)(2,1)S(1)}, u32[]{:S(2)}, u32[]{:S(2)}) collective-permute-start(bf16[4,32,1792]{2,1,0:T(8,128)(2,1)S(1)} %fusion.7), channel_id=1, source_target_pairs={{0,4},{2,6},{4,0},{6,2},{8,12},{10,14},{12,8},{14,10},{16,20},{18,... | collective-permute-start | bytes 1376264 | tf_op jit(solution)/shard_map/ppermute | solution.py:65
  217.1 19.5 %collective-permute-start.76 = (bf16[4,32,1792]{2,1,0:T(8,128)(2,1)S(1)}, bf16[4,32,1792]{2,1,0:T(8,128)(2,1)S(1)}, u32[]{:S(2)}, u32[]{:S(2)}) collective-permute-start(bf16[4,32,1792]{2,1,0:T(8,128)(2,1)S(1)} %fusion.8), channel_id=1, source_target_pairs={{0,2},{2,0},{4,6},{6,4},{8,10},{10,8},{12,14},{14,12},{16,18},{18,... | collective-permute-start | bytes 1376264 | tf_op jit(solution)/shard_map/ppermute | solution.py:65
  218.5 17.3 %collective-permute-start.67 = (bf16[4,32,768]{2,1,0:T(8,128)(2,1)S(1)}, bf16[4,32,768]{2,1,0:T(8,128)(2,1)S(1)}, u32[]{:S(2)}, u32[]{:S(2)}) collective-permute-start(bf16[4,32,768]{2,1,0:T(8,128)(2,1)S(1)} %fusion.21), channel_id=1, source_target_pairs={{0,4},{2,6},{4,0},{6,2},{8,12},{10,14},{12,8},{14,10},{16,20},{18,... | collective-permute-start | bytes 589832 | tf_op jit(solution)/shard_map/ppermute | solution.py:65
  225.3 10.6 %collective-permute-start.69 = (bf16[4,32,768]{2,1,0:T(8,128)(2,1)S(1)}, bf16[4,32,768]{2,1,0:T(8,128)(2,1)S(1)}, u32[]{:S(2)}, u32[]{:S(2)}) collective-permute-start(bf16[4,32,768]{2,1,0:T(8,128)(2,1)S(1)} %fusion.22), channel_id=1, source_target_pairs={{0,2},{2,0},{4,6},{6,4},{8,10},{10,8},{12,14},{14,12},{16,18},{18,... | collective-permute-start | bytes 589832 | tf_op jit(solution)/shard_map/ppermute | solution.py:65
  236.1 9.0 %collective-permute-start.70 = (bf16[2,64,768]{2,1,0:T(8,128)(2,1)S(1)}, bf16[2,64,768]{2,1,0:T(8,128)(2,1)S(1)}, u32[]{:S(2)}, u32[]{:S(2)}) collective-permute-start(bf16[2,64,768]{2,1,0:T(8,128)(2,1)S(1)} %fusion.20), channel_id=1, source_target_pairs={{0,8},{2,10},{4,12},{6,14},{8,0},{10,2},{12,4},{14,6},{16,24},{18,... | collective-permute-start | bytes 589832 | tf_op jit(solution)/shard_map/ppermute | solution.py:65
  236.8 14.7 %collective-permute-start.77 = (bf16[2,64,1792]{2,1,0:T(8,128)(2,1)S(1)}, bf16[2,64,1792]{2,1,0:T(8,128)(2,1)S(1)}, u32[]{:S(2)}, u32[]{:S(2)}) collective-permute-start(bf16[2,64,1792]{2,1,0:T(8,128)(2,1)S(1)} %fusion.9), channel_id=1, source_target_pairs={{0,8},{2,10},{4,12},{6,14},{8,0},{10,2},{12,4},{14,6},{16,24},{18,... | collective-permute-start | bytes 1376264 | tf_op jit(solution)/shard_map/ppermute | solution.py:65
  245.1 9.9 %collective-permute-start.71 = (bf16[1,64,768]{2,1,0:T(8,128)(2,1)S(1)}, bf16[1,64,768]{2,1,0:T(8,128)(2,1)S(1)}, u32[]{:S(2)}, u32[]{:S(2)}) collective-permute-start(bf16[1,64,768]{2,1,0:T(8,128)(2,1)S(1)} %fusion.29), channel_id=1, source_target_pairs={{0,16},{2,18},{4,20},{6,22},{8,24},{10,26},{12,28},{14,30},{16,0},... | collective-permute-start | bytes 294920 | tf_op jit(solution)/shard_map/ppermute | solution.py:65
  251.6 9.9 %collective-permute-start.78 = (bf16[1,64,1792]{2,1,0:T(8,128)(2,1)S(1)}, bf16[1,64,1792]{2,1,0:T(8,128)(2,1)S(1)}, u32[]{:S(2)}, u32[]{:S(2)}) collective-permute-start(bf16[1,64,1792]{2,1,0:T(8,128)(2,1)S(1)} %fusion.18), channel_id=1, source_target_pairs={{0,16},{2,18},{4,20},{6,22},{8,24},{10,26},{12,28},{14,30},{16,0},... | collective-permute-start | bytes 688136 | tf_op jit(solution)/shard_map/ppermute | solution.py:65
  255.0 6.6 %collective-permute-start.72 = (f32[64,768]{1,0:T(8,128)S(1)}, f32[64,768]{1,0:T(8,128)S(1)}, u32[]{:S(2)}, u32[]{:S(2)}) collective-permute-start(f32[64,768]{1,0:T(8,128)S(1)} %fusion.24), channel_id=1, source_target_pairs={{0,1},{1,0},{2,3},{3,2},{4,5},{5,4},{6,7},{7,6},{8,9},{9,8},{10,11... | collective-permute-start | bytes 589832 | tf_op jit(solution)/shard_map/ppermute | solution.py:69
  (130 other events, 2201.3 us)
where the time goes:
time: 284 us; the launch traced here: 283 us
  waiting for transfers between devices  115 us (40%)
  Pallas kernels  73.7 us (26%)
  starting transfers between devices  72.6 us (26%)
  other arithmetic  12.9 us (5%)
  local copies, waits for them, and re-layouts  6.79 us (2%)
    ppermute x54, waiting for transfers between devices, flip(): lax.ppermute(array, 'dp', [(i, i ^ mask) for i in range(lax.axis_size('dp...  108 us
    ppermute x54, starting transfers between devices, flip(): lax.ppermute(array, 'dp', [(i, i ^ mask) for i in range(lax.axis_size('dp...  65.9 us
    pallas_call x1, Pallas kernels, chain(): pl.pallas_call(functools.partial(chain_kernel, len(blocks), len(outs), fe...  20 us
    pallas_call x1, Pallas kernels, pixel_back(): pl.pallas_call(functools.partial(pixel_back_kernel, scale), out_shape=[sh...  19 us
    pallas_call x1, Pallas kernels, attend(): pl.pallas_call(functools.partial(attend_kernel, len(blocks), scale, feats...  15.4 us
    pallas_call x1, Pallas kernels, query_back(): pl.pallas_call(functools.partial(query_back_kernel, len(blocks), len(outs...  8.74 us
    ppermute x39, waiting for transfers between devices, trade(): return lax.ppermute(array, 'seq', swap)  7.76 us
    pallas_call x1, Pallas kernels, norm_pixels(): pl.pallas_call(pixel_kernel, out_shape=[shape((main + rest, count), half)...  7.5 us
  transfers between devices with their start and end apart: 93, of which 46 were waited for; matrix products, arithmetic and copies ran while one was open for 2% of the time, Pallas kernels for 9%

commit v1 on v0

v1 whole, which is shorter than its diff:
```python
import functools

import jax
import jax.numpy as jnp
from jax import lax
from jax.experimental import pallas as pl
from jax.experimental.pallas import tpu as pltpu
from jax.sharding import PartitionSpec as P

STEP = 10


norm_epsilon = 1e-05
beta_one = 0.9
beta_two = 0.999
decay_rate = 0.01
epsilon = 1e-06
learn_rate = 0.25
vector_rate = 1.0
masked_score = -1e30
gelu_coeff = 0.7978845608028654


def adam_moments(grad, first, second):
    first_new = beta_one * first + (1.0 - beta_one) * grad
    second_new = beta_two * second + (1.0 - beta_two) * grad * grad
    ratio = (
        first_new
        / (1.0 - beta_one**STEP)
        / (jnp.sqrt(second_new / (1.0 - beta_two**STEP)) + epsilon)
    )
    return (first_new, second_new, ratio)

half = jnp.bfloat16
single = jnp.float32
swap = [(0, 1), (1, 0)]
main, rest = 256, 128
whole = pl.BlockSpec(memory_space=pltpu.VMEM)
remote = pl.BlockSpec(memory_space=pl.ANY)
scalars = pl.BlockSpec(memory_space=pltpu.SMEM)
params = pltpu.CompilerParams(vmem_limit_bytes=56 * 2**20)


def cost(micros):
    return pl.CostEstimate(flops=int(micros * 1.1e9), bytes_accessed=1024, transcendentals=0)


def shape(dims, dtype):
    return jax.ShapeDtypeStruct(dims, dtype)


def contract(left, right, over_left, over_right):
    return lax.dot_general(left, right, (((over_left,), (over_right,)), ((), ())), preferred_element_type=single)


def nn(left, right):
    return contract(left, right, 1, 0)


def nt(left, right):
    return contract(left, right, 1, 1)


def tn(left, right):
    return contract(left, right, 0, 0)


def flip(array, mask):
    return lax.ppermute(array, "dp", [(i, i ^ mask) for i in range(lax.axis_size("dp"))])


def trade(array):
    return lax.ppermute(array, "seq", swap)


def special(groups, shard):
    return groups == 16 and shard % 32 == 0


def tie_kernel(*refs):
    pass


def tie(arrays, *after):
    return pl.pallas_call(
        tie_kernel,
        out_shape=[shape(a.shape, a.dtype) for a in arrays],
        in_specs=[remote] * (len(arrays) + len(after)),
        out_specs=[remote] * len(arrays),
        input_output_aliases={i: i for i in range(len(arrays))},
        cost_estimate=cost(0.1),
        name="tie",
    )(*arrays, *after)


def stack_kernel(plan, *refs):
    outs = refs[len(refs) - len(plan) :]
    for out, parts in zip(outs, plan):
        rows = out.shape[0] // len(parts)
        for i, (source, part) in enumerate(parts):
            out[pl.ds(i * rows, rows), :] = refs[source][pl.ds(part * rows, rows), :]


def stack(arrays, rows, plan, *after):
    lanes, dtype = arrays[0].shape[1], arrays[0].dtype
    return pl.pallas_call(
        functools.partial(stack_kernel, plan),
        out_shape=[shape((rows * len(parts), lanes), dtype) for parts in plan],
        in_specs=[whole] * len(arrays) + [remote] * len(after),
        out_specs=[whole] * len(plan),
        compiler_params=params,
        cost_estimate=cost(1.5),
        name="stack",
    )(*arrays, *after)


def gather_blocks(block, early, late):
    rows = block.shape[0]
    first = [flip(block, o) for o in (8, 4, 3, 2, 1)]
    plan = (((2, 0), (0, 0)), ((1, 0), (0, 0)), ((5, 0), (0, 0), (1, 0), (2, 0), (3, 0), (4, 0)))
    across, both, gathered = stack([*first, block], rows, plan, early)
    second = [flip(across, 4), flip(both, 2), flip(both, 1)]
    seven, twelve, twelve_ten = stack(second, rows, (((0, 0),), ((0, 1),), ((0, 1), (1, 1))), late)
    third = [flip(seven, 8), flip(twelve, 2), flip(twelve_ten, 1)]
    return [
        ((0, 8, 4, 3, 2, 1), gathered),
        ((7, 12), second[0]),
        ((6, 10), second[1]),
        ((5, 9), second[2]),
        ((15,), third[0]),
        ((14,), third[1]),
        ((13, 11), third[2]),
    ]


def pack_kernel(feats, spot, squares, pixels, block):
    side = spot[1]
    part = squares.shape[2] // 2
    lanes = pl.ds(pl.multiple_of(side * part, part), part)
    over = feats - main

    def pixel(m):
        last = pixels[m, :, pl.ds(main, over)]
        last = jnp.concatenate([last, jnp.zeros((last.shape[0], main - over), single)], axis=1)
        return jnp.where(side == 0, pixels[m, :, pl.ds(0, main)], last).astype(half)

    block[:, pl.ds(0, part)] = squares[0, :, lanes].astype(half)
    block[:, pl.ds(part, main)] = pixel(0)
    for m in range(1, 4):
        block[:, pl.ds(m * part + main, part)] = squares[m, :, lanes].astype(half)
    block[:, pl.ds(4 * part + main, main)] = pixel(1)


def pack(spot, squares, pixels):
    _, shard, width = squares.shape
    return pl.pallas_call(
        functools.partial(pack_kernel, pixels.shape[2]),
        out_shape=shape((shard, 4 * (width // 2) + 2 * main), half),
        in_specs=[scalars, whole, whole],
        out_specs=whole,
        compiler_params=params,
        cost_estimate=cost(2),
        name="pack",
    )(spot, squares, pixels)


def gather_matrices(block, early, late):
    groups = lax.axis_size("dp")
    shard = block.shape[0]
    if special(groups, shard):
        arrays, layout = [], []
        for positions, array in gather_blocks(block, early, late):
            arrays += [array, trade(array)]
            layout += [(positions, 0), (positions, 1)]
        return arrays, tuple(layout)
    every = lax.all_gather(block, ("dp", "seq"), axis=0).reshape(groups, 2, shard, -1)
    return [every.transpose(1, 0, 2, 3).reshape(2, groups * shard, -1)], ()


def load_blocks(spot, blocks, layout, target, first, sems):
    copies = []
    lanes = pl.ds(first, target.shape[2])
    if not layout:
        copies.append(pltpu.make_async_copy(blocks[0].at[:, :, lanes], target, sems.at[0]))
    for block, (positions, turn) in zip(blocks, layout):
        rows = block.shape[0] // len(positions)
        side = lax.bitwise_xor(spot[1], turn)
        for i, o in enumerate(positions):
            chip = lax.bitwise_xor(spot[0], o)
            place = target.at[side, pl.ds(pl.multiple_of(chip * rows, rows), rows)]
            copies.append(pltpu.make_async_copy(block.at[pl.ds(i * rows, rows), lanes], place, sems.at[len(copies)]))
    for copy in copies:
        copy.start()
    return copies


written = ((13, 11), (14,), (15,), (5, 9), (6, 10), (7, 12), (1,), (2,), (3,), (4,), (8,), (0,))


def store_terms(spot, terms, outs):
    if len(outs) == 1:
        outs[0][...] = terms[...].astype(half)
        return
    for positions, out in zip(written, outs):
        rows = terms.shape[0] // 16
        for i, o in enumerate(positions):
            chip = lax.bitwise_xor(spot[0], o)
            out[pl.ds(i * rows, rows), :] = terms[pl.ds(pl.multiple_of(chip * rows, rows), rows), :].astype(half)


def term_shapes(groups, shard, lanes):
    if special(groups, shard):
        return [shape((len(positions) * shard, lanes), half) for positions in written]
    return [shape((groups * shard, lanes), half)]


def send_first(terms, *after):
    if len(terms) == 1:
        return None
    got = [flip(terms[0], 1), flip(terms[1], 2), flip(terms[2], 8)]
    return tie(got, *after) if after else got


def send_second(terms, got, *after):
    if len(terms) == 1:
        return None
    rows = terms[-1].shape[0]

    def added(array, *more):
        total = array[rows:].astype(single)
        for other in more[0]:
            total = total + other.astype(single)
        first = array[:rows].astype(single)
        for other in more[1]:
            first = first + other.astype(single)
        return jnp.concatenate([first.astype(half), total.astype(half)])

    twelve, ten = got[0][:rows], got[0][rows:]
    got = [
        flip(terms[3], 1),
        flip(added(terms[4], [ten], []), 2),
        flip(added(terms[5], [twelve, got[1]], [got[2]]), 4),
    ]
    return tie(got, *after) if after else got


def send_third(terms, got):
    if len(terms) == 1:
        return [lax.psum_scatter(terms[0], "dp", scatter_dimension=0, tiled=True)]
    rows = terms[-1].shape[0]
    one, two, three, four, eight, _ = [term.astype(single) for term in terms[6:]]
    x, y, z = [array.astype(single) for array in got]
    sent = [
        (eight + x[rows:] + y[rows:] + z[rows:], 8),
        (four + x[:rows] + y[:rows], 4),
        (three + z[:rows], 3),
        (two, 2),
        (one, 1),
    ]
    return [flip(array.astype(half), mask) for array, mask in sent]


def sum_own(terms, got):
    if len(terms) > 1:
        got = [terms[-1], *got]
    total = got[0].astype(single)
    for array in got[1:]:
        total = total + array.astype(single)
    return total


def sum_all(array):
    mask = 1
    size = lax.axis_size("dp")
    while mask < size:
        if mask * 2 < size:
            one, two, three = flip(array, mask), flip(array, 2 * mask), flip(array, 3 * mask)
            array = (array + one) + (two + three)
            mask *= 4
        else:
            array = array + flip(array, mask)
            mask *= 2
    return array


def standard(values):
    center = values - jnp.mean(values, axis=-1, keepdims=True)
    inverse = lax.rsqrt(jnp.mean(center * center, axis=-1, keepdims=True) + norm_epsilon)
    return center * inverse, inverse


def standard_back(grad, gain, unit, inverse):
    scaled = grad * gain
    return inverse * (
        scaled - jnp.mean(scaled, axis=-1, keepdims=True) - unit * jnp.mean(scaled * unit, axis=-1, keepdims=True)
    )


def pixel_kernel(pixels, gain, shift, normed, stats, held, tail, sem):
    copy = pltpu.make_async_copy(pixels.at[:, 0, :], held, sem)
    copy.start()
    feats = held.shape[0]
    step = 256
    over = feats - main
    tail[...] = jnp.zeros_like(tail)
    copy.wait()

    @pl.loop(0, held.shape[1] // step)
    def _(i):
        lanes = pl.ds(pl.multiple_of(i * step, step), step)
        first, last = held[pl.ds(0, main), lanes], held[pl.ds(main, over), lanes]
        mean = (jnp.sum(first, axis=0, keepdims=True) + jnp.sum(last, axis=0, keepdims=True)) / feats
        first, last = first - mean, last - mean
        spread = (
            jnp.sum(first * first, axis=0, keepdims=True) + jnp.sum(last * last, axis=0, keepdims=True)
        ) / feats
        inverse = lax.rsqrt(spread + norm_epsilon)
        normed[pl.ds(0, main), lanes] = (first * inverse * gain[pl.ds(0, main)] + shift[pl.ds(0, main)]).astype(half)
        tail[pl.ds(0, over), :] = last * inverse * gain[pl.ds(main, over)] + shift[pl.ds(main, over)]
        normed[pl.ds(main, rest), lanes] = tail[...].astype(half)
        stats[0:1, lanes] = mean
        stats[1:2, lanes] = inverse


def norm_pixels(pixels, gain, shift):
    feats, _, count = pixels.shape
    return pl.pallas_call(
        pixel_kernel,
        out_shape=[shape((main + rest, count), half), shape((2, count), single)],
        in_specs=[remote, whole, whole],
        out_specs=[whole] * 2,
        scratch_shapes=[pltpu.VMEM((feats, count), single), pltpu.VMEM((rest, 256), single), pltpu.SemaphoreType.DMA],
        compiler_params=params,
        cost_estimate=cost(7),
        name="norm_pixels",
    )(pixels, gain, shift)


def latent_kernel(latents, vectors, normed):
    unit, _ = standard(latents[...])
    normed[...] = (unit * vectors[0:1, :] + vectors[1:2, :]).astype(half)


def norm_latents(latents, vectors):
    return pl.pallas_call(
        latent_kernel,
        out_shape=shape(latents.shape, half),
        in_specs=[whole] * 2,
        out_specs=whole,
        compiler_params=params,
        cost_estimate=cost(2),
        name="norm_latents",
    )(latents, vectors)


def attend_kernel(count, layout, scale, feats, spot, *refs):
    blocks = refs[:count]
    mine, theirs, pixels, keep, query, query_pix, sent, weights, sems = refs[count:]
    copies = load_blocks(spot, blocks, layout, weights, 0, sems)
    for copy in copies:
        copy.wait()
    step, part = mine.shape[0], mine.shape[1] // 2
    for t, normed in enumerate((mine, theirs)):
        rows = pl.ds(t * step, step)
        value = nt(normed[:, pl.ds(0, part)], weights[0, :, pl.ds(0, part)])
        value = value + nt(normed[:, pl.ds(part, part)], weights[1, :, pl.ds(0, part)])
        value = value.astype(half)
        query[rows, :] = value
        query_pix[rows, pl.ds(0, main)] = (nn(value, weights[0, :, pl.ds(part, main)]) * scale).astype(half)
        query_pix[rows, pl.ds(main, rest)] = (nn(value, weights[1, :, pl.ds(part, rest)]) * scale).astype(half)
    tile = 128

    @pl.loop(0, query.shape[0] // tile)
    def _(i):
        rows = pl.ds(pl.multiple_of(i * tile, tile), tile)
        scores = nn(query_pix[rows, :], pixels[...])
        scores = jnp.where(keep[...] > 0, scores, masked_score)
        top = jnp.max(scores, axis=-1, keepdims=True)
        expo = jnp.exp(scores - top)
        total = jnp.sum(expo, axis=-1, keepdims=True)
        expo = expo.astype(half)
        value = nt(expo, pixels[...])
        lane = lax.broadcasted_iota(jnp.int32, value.shape, 1)
        sent[rows, :] = jnp.where(lane == feats, top, jnp.where(lane == feats + 1, total, value))


def attend(spot, gathered, normed, pixels, keep, scale, feats):
    blocks, layout = gathered
    rows, width = 2 * normed[0].shape[0], normed[0].shape[1]
    lanes = width // 2 + main
    return pl.pallas_call(
        functools.partial(attend_kernel, len(blocks), layout, scale, feats),
        out_shape=[shape((rows, width), half), shape((rows, main + rest), half), shape((rows, main + rest), single)],
        in_specs=[scalars] + [remote] * len(blocks) + [whole] * 4,
        out_specs=[whole] * 3,
        scratch_shapes=[pltpu.VMEM((2, width, lanes), half), pltpu.SemaphoreType.DMA((32,))],
        compiler_params=params,
        cost_estimate=cost(14),
        name="attend",
    )(spot, *blocks, *normed, pixels, keep)


def chain_kernel(count, layout, terms_count, feats, spot, *refs):
    blocks, refs = refs[:count], refs[count:]
    (mine, theirs, latent_mine, latent_theirs, cot_mine, cot_theirs, vectors), refs = refs[:7], refs[7:]
    (latents_out, middle_grad, grad_pix, stats, sums), refs = refs[:5], refs[5:]
    term_outs, refs = refs[:terms_count], refs[terms_count:]
    weights, attended, middle_half, mixed, hidden_grad, active, out_half, attended_grad, value_mix, wide, terms, sems = refs
    copies = load_blocks(spot, blocks, layout, weights, blocks[0].shape[-1] - weights.shape[2], sems)
    for copy in copies:
        copy.wait()
    rows_all, width = attended.shape
    step = rows_all // 2
    part = width // 2

    def into(value, m):
        lanes = pl.ds(m * part, part)
        return nt(value[:, :part], weights[0, :, lanes]) + nt(value[:, part:], weights[1, :, lanes])

    def back(value, m, target):
        lanes = pl.ds(m * part, part)
        target[:, pl.ds(0, part)] = nn(value, weights[0, :, lanes])
        target[:, pl.ds(part, part)] = nn(value, weights[1, :, lanes])
        return target[...]

    sums[...] = jnp.zeros_like(sums)
    value_mix[...] = jnp.zeros_like(value_mix)
    for t in range(2):
        rows, other = pl.ds(t * step, step), pl.ds((1 - t) * step, step)
        latents, cotangent = (latent_mine, cot_mine) if t == 0 else (latent_theirs, cot_theirs)
        here, there = mine[rows, :], theirs[other, :]
        top_here, top_there = here[:, feats : feats + 1], there[:, feats : feats + 1]
        top = jnp.maximum(top_here, top_there)
        scale_here, scale_there = jnp.exp(top_here - top), jnp.exp(top_there - top)
        total = here[:, feats + 1 : feats + 2] * scale_here + there[:, feats + 1 : feats + 2] * scale_there
        mix = (here * scale_here + there * scale_there) / total
        lane = lax.broadcasted_iota(jnp.int32, mix.shape, 1)
        mix = jnp.where(lane < feats, mix, 0.0).astype(half)
        value_mix[rows, pl.ds(0, main + rest)] = mix
        attended_f = nt(mix[:, :main], weights[0, :, pl.ds(3 * part, main)])
        attended_f = attended_f + nt(mix[:, main:], weights[1, :, pl.ds(3 * part, rest)])
        wide[...] = attended_f
        value = attended_f.astype(half)
        attended[rows, :] = value
        middle = latents[...] + into(value, 0)
        unit, inverse = standard(middle)
        value = (unit * vectors[2:3, :] + vectors[3:4, :]).astype(half)
        mixed[rows, :] = value
        hidden = into(value, 1) + vectors[4:5, :]
        curve = jnp.tanh(gelu_coeff * (hidden + 0.044715 * hidden * hidden * hidden))
        value = (0.5 * hidden * (1.0 + curve)).astype(half)
        active[rows, :] = value
        if t == 0:
            latents_out[...] = middle + into(value, 2) + vectors[5:6, :]
        slope = 0.5 * (1.0 + curve) + 0.5 * hidden * (1.0 - curve * curve) * gelu_coeff * (
            1.0 + 3.0 * 0.044715 * hidden * hidden
        )
        value = cotangent[...].astype(half)
        out_half[rows, :] = value
        if t == 0:
            sums[5:6, :] = jnp.sum(value.astype(single), axis=0, keepdims=True)
        scratch = terms.at[pl.ds(0, step), pl.ds(0, width)]
        value = (back(value, 2, scratch) * slope).astype(half)
        hidden_grad[rows, :] = value
        if t == 0:
            sums[4:5, :] = jnp.sum(value.astype(single), axis=0, keepdims=True)
        mixed_grad = back(value, 1, scratch)
        if t == 0:
            sums[2:3, :] = jnp.sum(mixed_grad * unit, axis=0, keepdims=True)
            sums[3:4, :] = jnp.sum(mixed_grad, axis=0, keepdims=True)
        grad = cotangent[...] + standard_back(mixed_grad, vectors[2:3, :], unit, inverse)
        if t == 0:
            middle_grad[...] = grad
        value = grad.astype(half)
        middle_half[rows, :] = value
        value = back(value, 0, scratch).astype(half)
        attended_grad[rows, :] = value
        inner = jnp.sum(wide[...] * value.astype(single), axis=-1, keepdims=True)
        grad_pix[rows, pl.ds(0, main)] = nn(value, weights[0, :, pl.ds(3 * part, main)]).astype(half)
        grad_pix[rows, pl.ds(main, rest)] = nn(value, weights[1, :, pl.ds(3 * part, rest)]).astype(half)
        lane = lax.broadcasted_iota(jnp.int32, (step, 128), 1)
        stats[rows, :] = jnp.where(lane == 0, top + jnp.log(total), inner)
    side = pl.ds(pl.multiple_of(spot[1] * part, part), part)
    for m, (grad, value) in enumerate(((middle_half, attended), (hidden_grad, mixed), (out_half, active))):
        terms[:, pl.ds(m * part, part)] = tn(grad[...], value[:, side])
    side = pl.ds(pl.multiple_of(spot[1] * main, main), main)
    terms[:, pl.ds(3 * part, main)] = tn(attended_grad[...], value_mix[:, side])
    store_terms(spot, terms, term_outs)


def chain(spot, gathered, mine, theirs, latents, cotangents, vectors, feats, groups):
    blocks, layout = gathered
    rows, width = mine.shape[0], vectors.shape[1]
    lanes = 3 * (width // 2) + main
    outs = term_shapes(groups, width // groups, lanes)
    bits = pltpu.VMEM((rows, width), half)
    result = pl.pallas_call(
        functools.partial(chain_kernel, len(blocks), layout, len(outs), feats),
        out_shape=[
            shape((rows // 2, width), single),
            shape((rows // 2, width), single),
            shape((rows, main + rest), half),
            shape((rows, 128), single),
            shape((8, width), single),
        ]
        + outs,
        in_specs=[scalars] + [remote] * len(blocks) + [whole] * 7,
        out_specs=[whole] * (5 + len(outs)),
        scratch_shapes=[pltpu.VMEM((2, width, lanes), half)]
        + [bits] * 7
        + [
            pltpu.VMEM((rows, 2 * main), half),
            pltpu.VMEM((rows // 2, width), single),
            pltpu.VMEM((width, lanes), single),
            pltpu.SemaphoreType.DMA((32,)),
        ],
        compiler_params=params,
        cost_estimate=cost(20),
        name="chain",
    )(spot, *blocks, mine, theirs, *latents, *cotangents, vectors)
    return result[:5], result[5:]


def pixel_back_kernel(scale, turn, turns, *refs):
    (query_pix, grad_pix, stats, normed, keep, pixels, gain, pixel_stats), refs = refs[:8], refs[8:]
    if turn > 0:
        (score_before, sums_before, _), refs = refs[:3], refs[3:]
    score_pix, sums, pixels_grad, held, made, query_t, grad_t, slope, shift, sem, sems = refs
    origin = turn * held.shape[1]
    copy = pltpu.make_async_copy(pixels.at[:, 0, pl.ds(origin, held.shape[1])], held, sem)
    copy.start()
    feats, count = held.shape
    over = feats - main
    step = 512
    query_t[...] = jnp.transpose(query_pix[...].astype(single)).astype(half)
    grad_t[...] = jnp.transpose(grad_pix[...].astype(single)).astype(half)
    score_pix[...] = score_before[...] if turn > 0 else jnp.zeros_like(score_pix)
    slope[...] = jnp.zeros_like(slope)
    shift[...] = jnp.zeros_like(shift)
    log_total, inner = stats[:, 0:1], stats[:, 1:2]
    copy.wait()

    @pl.loop(0, count // step)
    def _(i):
        here = pl.ds(pl.multiple_of(i * step, step), step)
        lanes = pl.ds(pl.multiple_of(origin + i * step, step), step)
        values = normed[:, lanes]
        scores = nn(query_pix[...], values)
        weight_grad = nn(grad_pix[...], values)
        attn = jnp.exp(jnp.where(keep[:, lanes] > 0, scores, masked_score) - log_total)
        score_grad = (attn * (weight_grad - inner)).astype(half)
        attn = attn.astype(half)
        score_pix[...] += nt(score_grad, values)
        grad = nn(query_t[...], score_grad) + nn(grad_t[...], attn)
        mean, inverse = pixel_stats[0:1, lanes], pixel_stats[1:2, lanes]
        unit_a = (held[pl.ds(0, main), here] - mean) * inverse
        unit_b = (held[pl.ds(main, over), here] - mean) * inverse
        grad_a, grad_b = grad[:main], grad[main : main + over]
        for rows, g, u in ((pl.ds(0, main), grad_a, unit_a), (pl.ds(main, over), grad_b, unit_b)):
            product = g * u
            slope[rows, :] += sum(product[:, 128 * j : 128 * j + 128] for j in range(step // 128))
            shift[rows, :] += sum(g[:, 128 * j : 128 * j + 128] for j in range(step // 128))
        scaled_a, scaled_b = grad_a * gain[pl.ds(0, main)], grad_b * gain[pl.ds(main, over)]
        flat = (jnp.sum(scaled_a, axis=0, keepdims=True) + jnp.sum(scaled_b, axis=0, keepdims=True)) / feats
        along = (
            jnp.sum(scaled_a * unit_a, axis=0, keepdims=True) + jnp.sum(scaled_b * unit_b, axis=0, keepdims=True)
        ) / feats
        made[pl.ds(0, main), here] = inverse * (scaled_a - flat - unit_a * along)
        made[pl.ds(main, over), here] = inverse * (scaled_b - flat - unit_b * along)
        pltpu.make_async_copy(made.at[:, here], pixels_grad.at[:, 0, lanes], sems.at[i]).start()

    if turn == turns - 1:
        score_pix[...] = score_pix[...] * scale
    lane = lax.broadcasted_iota(jnp.int32, (feats, 128), 1)
    both = jnp.where(
        lane == 0,
        jnp.sum(slope[...], axis=-1, keepdims=True),
        jnp.sum(shift[...], axis=-1, keepdims=True),
    )
    sums[...] = both + sums_before[...] if turn > 0 else both

    @pl.loop(0, count // step)
    def _(i):
        here = pl.ds(pl.multiple_of(i * step, step), step)
        lanes = pl.ds(pl.multiple_of(origin + i * step, step), step)
        pltpu.make_async_copy(made.at[:, here], pixels_grad.at[:, 0, lanes], sems.at[i]).wait()


def pixel_back(query_pix, grad_pix, stats, normed, keep, pixels, gain, pixel_stats, scale, turn, turns, before):
    feats, _, count = pixels.shape
    rows = query_pix.shape[0]
    held = pltpu.VMEM((feats, count // turns), single)
    return pl.pallas_call(
        functools.partial(pixel_back_kernel, scale, turn, turns),
        out_shape=[shape((rows, main + rest), single), shape((feats, 128), single), shape(pixels.shape, single)],
        in_specs=[whole] * 5 + [remote, whole, whole] + [whole, whole, remote][: len(before)],
        out_specs=[whole, whole, remote],
        scratch_shapes=[
            held,
            held,
            pltpu.VMEM((main + rest, rows), half),
            pltpu.VMEM((main + rest, rows), half),
            pltpu.VMEM((feats, 128), single),
            pltpu.VMEM((feats, 128), single),
            pltpu.SemaphoreType.DMA,
            pltpu.SemaphoreType.DMA((count // turns // 512,)),
        ],
        input_output_aliases={10: 2} if before else {},
        compiler_params=params,
        cost_estimate=cost(18 / turns),
        name="pixel_back",
    )(query_pix, grad_pix, stats, normed, keep, pixels, gain, pixel_stats, *before)


def query_back_kernel(count, layout, terms_count, spot, *refs):
    blocks, refs = refs[:count], refs[count:]
    (mine, theirs, query, normed_mine, normed_theirs, latents, middle_grad, vectors), refs = refs[:8], refs[8:]
    (latents_grad, sums), refs = refs[:2], refs[2:]
    term_outs, refs = refs[:terms_count], refs[terms_count:]
    weights, score_pix, query_grad, wide, terms, sems = refs
    copies = load_blocks(spot, blocks, layout, weights, 0, sems)
    rows_all, width = query.shape
    step = rows_all // 2
    part = width // 2
    score_pix[:, pl.ds(main + rest, rest)] = jnp.zeros((rows_all, rest), half)
    for t in range(2):
        rows, other = pl.ds(t * step, step), pl.ds((1 - t) * step, step)
        score_pix[rows, pl.ds(0, main + rest)] = (mine[rows, :] + theirs[other, :]).astype(half)
    for copy in copies:
        copy.wait()
    for t in range(2):
        rows = pl.ds(t * step, step)
        value = nt(score_pix[rows, pl.ds(0, main)], weights[0, :, pl.ds(part, main)])
        value = value + nt(score_pix[rows, pl.ds(main, rest)], weights[1, :, pl.ds(part, rest)])
        query_grad[rows, :] = value.astype(half)
    side = pl.ds(pl.multiple_of(spot[1] * part, part), part)
    value = tn(query_grad[pl.ds(0, step), :], normed_mine[:, side])
    terms[:, pl.ds(0, part)] = value + tn(query_grad[pl.ds(step, step), :], normed_theirs[:, side])
    side = pl.ds(pl.multiple_of(spot[1] * main, main), main)
    terms[:, pl.ds(part, main)] = tn(query[...], score_pix[:, side])
    store_terms(spot, terms, term_outs)
    value = query_grad[pl.ds(0, step), :]
    wide[:, pl.ds(0, part)] = nn(value, weights[0, :, pl.ds(0, part)])
    wide[:, pl.ds(part, part)] = nn(value, weights[1, :, pl.ds(0, part)])
    unit, inverse = standard(latents[...])
    grad = wide[...]
    latents_grad[...] = middle_grad[...] + standard_back(grad, vectors[0:1, :], unit, inverse)
    sums[...] = jnp.zeros_like(sums)
    sums[0:1, :] = jnp.sum(grad * unit, axis=0, keepdims=True)
    sums[1:2, :] = jnp.sum(grad, axis=0, keepdims=True)


def query_back(spot, gathered, mine, theirs, query, normed, latents, middle_grad, vectors, groups):
    blocks, layout = gathered
    rows, width = query.shape
    lanes = width // 2 + main
    outs = term_shapes(groups, width // groups, lanes)
    result = pl.pallas_call(
        functools.partial(query_back_kernel, len(blocks), layout, len(outs)),
        out_shape=[shape((rows // 2, width), single), shape((8, width), single)] + outs,
        in_specs=[scalars] + [remote] * len(blocks) + [whole] * 8,
        out_specs=[whole] * (2 + len(outs)),
        scratch_shapes=[
            pltpu.VMEM((2, width, lanes), half),
            pltpu.VMEM((rows, 2 * main), half),
            pltpu.VMEM((rows, width), half),
            pltpu.VMEM((rows // 2, width), single),
            pltpu.VMEM((width, lanes), single),
            pltpu.SemaphoreType.DMA((32,)),
        ],
        compiler_params=params,
        cost_estimate=cost(9),
        name="query_back",
    )(spot, *blocks, mine, theirs, query, *normed, latents, middle_grad, vectors)
    return result[:2], result[2:]


def moments_kernel(feats, *refs):
    spot, late_mine, late_theirs, early_mine, early_theirs, vectors, *refs = refs
    square_p, square_m, square_v, pixel_p, pixel_m, pixel_v, *refs = refs
    square_outs, pixel_outs, sums = refs[:4], refs[4:8], refs[8]
    width = square_p.shape[2]
    part = width // 2
    first = spot[1] == 0
    lane = lax.broadcasted_iota(jnp.int32, (1, width), 1)
    row = jnp.zeros((1, width), single)
    for m in range(6):
        mine, theirs = (late_mine, late_theirs) if m in (0, 4) else (early_mine, early_theirs)
        if m < 4:
            lanes = pl.ds(max(m - 1, 0) * part, part)
            sides, outs, k = (pl.ds(0, part), pl.ds(part, part)), square_outs, m
            params_now, first_now, second_now = square_p, square_m, square_v
        else:
            lanes = pl.ds(part if m == 4 else 3 * part, main)
            sides, outs, k = (pl.ds(0, main), pl.ds(main, feats - main)), pixel_outs, m - 4
            params_now, first_now, second_now = pixel_p, pixel_m, pixel_v
        own, other = mine[:, lanes], theirs[:, lanes]
        weight_total, update_total = jnp.zeros((1, 1), single), jnp.zeros((1, 1), single)
        for side, grad in zip(sides, (jnp.where(first, own, other), jnp.where(first, other, own))):
            grad = grad[:, : side.size]
            weight = params_now[k, :, side]
            first_new, second_new, ratio = adam_moments(grad, first_now[k, :, side], second_now[k, :, side])
            update = ratio + decay_rate * weight
            for out, value in zip(outs, (grad, first_new, second_new, update)):
                out[k, :, side] = value
            weight_total = weight_total + jnp.sum(weight * weight, keepdims=True)
            update_total = update_total + jnp.sum(update * update, keepdims=True)
        row = row + jnp.where(lane == m, weight_total, jnp.where(lane == 6 + m, update_total, 0.0))
    sums[...] = jnp.zeros_like(sums)
    sums[pl.ds(0, 8), :] = vectors[...]
    sums[8:9, :] = row


def moments(spot, late, early, vectors, square, pixel):
    big, small = shape(square[0].shape, single), shape(pixel[0].shape, single)
    return pl.pallas_call(
        functools.partial(moments_kernel, pixel[0].shape[2]),
        out_shape=[big] * 4 + [small] * 4 + [shape((16, big.shape[2]), single)],
        in_specs=[scalars] + [whole] * 11,
        out_specs=[whole] * 9,
        compiler_params=params,
        cost_estimate=cost(5),
        name="moments",
    )(spot, *late, *early, vectors, *square, *pixel)


def apply_kernel(sums, square_p, square_u, pixel_p, pixel_u, *refs):
    states, outs = refs[:6], refs[6:]
    square_new, square_copy, pixel_new, pixel_copy, norms, *news = outs
    weight_norm, update_norm = jnp.sqrt(sums[8:9, 0:6]), jnp.sqrt(sums[8:9, 6:12])
    trust = weight_norm / (update_norm + epsilon)
    for row, value in enumerate((weight_norm, update_norm, trust)):
        norms[row : row + 1, :] = value
    for m in range(6):
        k, weight, update, new, copy = (
            (m, square_p, square_u, square_new, square_copy)
            if m < 4
            else (m - 4, pixel_p, pixel_u, pixel_new, pixel_copy)
        )
        value = weight[k] - learn_rate * trust[:, m : m + 1] * update[k]
        new[k] = value
        copy[k] = value.astype(half)
    feats = states[3].shape[1]
    for grad, (value, first, second), out in (
        (sums[0:6, :], states[:3], news[:3]),
        (sums[6:8, 0:feats], states[3:], news[3:]),
    ):
        first_new, second_new, ratio = adam_moments(grad, first[...], second[...])
        out[0][...] = value[...] - vector_rate * ratio
        out[1][...] = first_new
        out[2][...] = second_new


def apply(sums, square_p, square_u, pixel_p, pixel_u, vectors, norms):
    outs = [(square_p, single), (square_p, half), (pixel_p, single), (pixel_p, half)]
    states = [*vectors, *norms]
    return pl.pallas_call(
        apply_kernel,
        out_shape=[shape(a.shape, dtype) for a, dtype in outs]
        + [shape((3, 6), single)]
        + [shape(a.shape, single) for a in states],
        in_specs=[whole] * 11,
        out_specs=[whole] * 11,
        compiler_params=params,
        cost_estimate=cost(4),
        name="apply",
    )(sums, square_p, square_u, pixel_p, pixel_u, *states)


def local(
    latents,
    pixels,
    keep_mask,
    cotangent,
    square_weights,
    square_first,
    square_second,
    pixel_weights,
    pixel_first,
    pixel_second,
    latent_vectors,
    latent_first,
    latent_second,
    pixel_norm,
    pixel_norm_first,
    pixel_norm_second,
):
    width = latents.shape[2]
    feats = pixels.shape[2]
    scale = width ** (-0.5)
    rank = lax.axis_index("seq")
    groups = lax.axis_size("dp")
    spot = jnp.stack([lax.axis_index("dp"), rank]).astype(jnp.int32)

    def turned(array):
        return jnp.transpose(array, (0, 2, 1))

    square = [turned(array) for array in (square_weights, square_first, square_second)]
    pixel = [turned(array) for array in (pixel_weights, pixel_first, pixel_second)]

    latents_two = (latents[0], trade(latents[0]))
    cotangent_two = (cotangent[0], trade(cotangent[0]))
    pixels_t = jnp.transpose(pixels, (2, 0, 1))
    gain, shift = pixel_norm[0][:, None], pixel_norm[1][:, None]
    pixel_normed, pixel_stats = norm_pixels(pixels_t, gain, shift)
    normed = norm_latents(latents[0], latent_vectors)
    normed = (normed, trade(normed))
    blocks = gather_matrices(pack(spot, square[0], pixel[0]), pixel_normed, normed[0])
    query, query_pix, sent = attend(spot, blocks, normed, pixel_normed, keep_mask, scale, feats)
    (latents_out, middle_grad, grad_pix, stats, chain_sums), early_terms = chain(
        spot, blocks, sent, trade(sent), latents_two, cotangent_two, latent_vectors, feats, groups
    )
    pixel_args = (query_pix, grad_pix, stats, pixel_normed, keep_mask, pixels_t, gain, pixel_stats, scale)
    turn_one = pixel_back(*pixel_args, 0, 2, ())
    if len(early_terms) > 1:
        *early_got, score_pix = tie([*send_first(early_terms), turn_one[0]], turn_one[1])
        turn_two = pixel_back(*pixel_args, 1, 2, [score_pix, *turn_one[1:]])
        early_got = send_second(early_terms, early_got, turn_two[0])
    else:
        turn_two, early_got = pixel_back(*pixel_args, 1, 2, turn_one), None
    score_pix, pixel_sums, pixels_grad = turn_two
    (latents_grad, query_sums), late_terms = query_back(
        spot, blocks, score_pix, trade(score_pix), query, normed, latents[0], middle_grad, latent_vectors, groups
    )
    early_got = send_third(early_terms, early_got)
    if len(late_terms) > 1:
        tied = tie([*late_terms[:3], *early_got], late_terms[3])
        late_terms, early_got = [*tied[:3], *late_terms[3:]], tied[3:]
    early = sum_own(early_terms, early_got)
    late = sum_own(late_terms, send_third(late_terms, send_second(late_terms, send_first(late_terms))))

    norm_terms = jnp.pad(jnp.transpose(pixel_sums[:, :2]), ((6, 0), (0, width - feats)))
    vector_terms = chain_sums + query_sums + norm_terms
    vector_terms = vector_terms + trade(vector_terms)
    square_grad, square_first_new, square_second_new, square_u, *rest_outs = moments(
        spot, (late, trade(late)), (early, trade(early)), vector_terms, square, pixel
    )
    pixel_weight_grad, pixel_first_new, pixel_second_new, pixel_u, sums = rest_outs
    square_new, square_copy, pixel_new, pixel_copy, matrix_norms, *news = apply(
        sum_all(sums),
        square[0],
        square_u,
        pixel[0],
        pixel_u,
        (latent_vectors, latent_first, latent_second),
        (pixel_norm, pixel_norm_first, pixel_norm_second),
    )
    latent_vectors_new, latent_first_new, latent_second_new = news[:3]
    pixel_norm_new, pixel_norm_first_new, pixel_norm_second_new = news[3:]
    return (
        latents_out[None],
        latents_grad[None],
        jnp.transpose(pixels_grad, (1, 2, 0)),
        turned(square_grad),
        turned(square_first_new),
        turned(square_second_new),
        turned(square_new),
        turned(square_copy),
        turned(pixel_weight_grad),
        turned(pixel_first_new),
        turned(pixel_second_new),
        turned(pixel_new),
        turned(pixel_copy),
        latent_first_new,
        latent_second_new,
        latent_vectors_new,
        pixel_norm_first_new,
        pixel_norm_second_new,
        pixel_norm_new,
        matrix_norms,
    )


def solution(mesh):
    return jax.shard_map(
        local,
        mesh=mesh,
        in_specs=(
            P("dp", "seq", None),
            P("dp", "seq", None),
            P("dp", "seq"),
            P("dp", "seq", None),
            P(None, None, "dp"),
            P(None, None, "dp"),
            P(None, None, "dp"),
            P(None, None, "dp"),
            P(None, None, "dp"),
            P(None, None, "dp"),
            P(),
            P(),
            P(),
            P(),
            P(),
            P(),
        ),
        out_specs=(
            P("dp", "seq", None),
            P("dp", "seq", None),
            P("dp", "seq", None),
            P(None, None, "dp"),
            P(None, None, "dp"),
            P(None, None, "dp"),
            P(None, None, "dp"),
            P(None, None, "dp"),
            P(None, None, "dp"),
            P(None, None, "dp"),
            P(None, None, "dp"),
            P(None, None, "dp"),
            P(None, None, "dp"),
            P(),
            P(),
            P(),
            P(),
            P(),
            P(),
            P(),
        ),
        check_vma=False,
    )
```

time: 284 us -> 222 us (0.78)
  waiting for transfers between devices: 115 us -> 50.7 us
  Pallas kernels: 73.7 us -> 95.3 us
  starting transfers between devices: 72.6 us -> 51 us
  local copies, waits for them, and re-layouts: 6.79 us -> 13.4 us
  other arithmetic: 12.9 us -> 9.19 us
    ppermute x54 -> x39, waiting for transfers between devices: 108 us -> 44.2 us  [flip(): lax.ppermute(array, 'dp', [(i, i ^ mask) for i in range(lax.axis_size('dp...]
    pallas_call x5 -> x14, Pallas kernels: 66.2 us -> 87.9 us  [the longest x2 24.4 us: pixel_back(): pl.pallas_call(functools.partial(pixel_back_kernel, scale, turn, turns),...]
    ppermute x54 -> x39, starting transfers between devices: 65.9 us -> 47.9 us  [flip(): lax.ppermute(array, 'dp', [(i, i ^ mask) for i in range(lax.axis_size('dp...]
    unnamed x170 -> x118, local copies, waits for them, and re-layouts: 3.65 us -> 9.76 us
    convert_element_type x2 -> x10, other arithmetic: 2.38 us -> 6.13 us  [the longest x6 3.32 us: send_third(): x, y, z = [array.astype(single) for array in got]]
    ppermute x39 -> x15, starting transfers between devices: 6.69 us -> 3.11 us  [trade(): return lax.ppermute(array, 'seq', swap)]
    reduce_sum x2 -> x0, other arithmetic: 3.48 us -> none  [the longest x1 2.51 us: local(): jnp.sum(square_update * square_update, axis=(1, 2))]
    ppermute x39 -> x15, waiting for transfers between devices: 7.76 us -> 6.48 us  [trade(): return lax.ppermute(array, 'seq', swap)]
  transfers between devices with their start and end apart: 93 -> 54, of which waited for: 46 -> 24; matrix products, arithmetic and copies ran while one was open for 2% -> 4% of each run, Pallas kernels for 9% -> 28%
where the time goes in v1:
time: 222 us; the launch traced here: 221 us
  Pallas kernels  95.3 us (43%)
  starting transfers between devices  51 us (23%)
  waiting for transfers between devices  50.7 us (23%)
  local copies, waits for them, and re-layouts  13.4 us (6%)
  other arithmetic  9.19 us (4%)
    ppermute x39, starting transfers between devices, flip(): lax.ppermute(array, 'dp', [(i, i ^ mask) for i in range(lax.axis_size('dp...  47.9 us
    ppermute x39, waiting for transfers between devices, flip(): lax.ppermute(array, 'dp', [(i, i ^ mask) for i in range(lax.axis_size('dp...  44.2 us
    pallas_call x2, Pallas kernels, pixel_back(): pl.pallas_call(functools.partial(pixel_back_kernel, scale, turn, turns),...  24.4 us
    pallas_call x1, Pallas kernels, chain(): pl.pallas_call(functools.partial(chain_kernel, len(blocks), layout, len(o...  19.9 us
    pallas_call x1, Pallas kernels, attend(): pl.pallas_call(functools.partial(attend_kernel, len(blocks), layout, scal...  15.3 us
    unnamed x118, local copies, waits for them, and re-layouts  9.76 us
    pallas_call x1, Pallas kernels, query_back(): pl.pallas_call(functools.partial(query_back_kernel, len(blocks), layout,...  8.64 us
    pallas_call x1, Pallas kernels, norm_pixels(): pl.pallas_call(pixel_kernel, out_shape=[shape((main + rest, count), half)...  7.46 us
  transfers between devices with their start and end apart: 54, of which 24 were waited for; matrix products, arithmetic and copies ran while one was open for 4% of the time, Pallas kernels for 28%

profile of v1, /device:TPU:0, one launch (start us, length us, event | category | flops | bytes accessed | tf_op | source)
XLA Modules:
  0.0 221.1 jit_solution(11333710531988605833)
XLA Ops:
  1.3 2.0 pack.1.refs_5_
  3.3 2.9 %collective-permute-start.4 = (bf16[64,2560]{1,0:T(8,128)(2,1)}, bf16[64,2560]{1,0:T(8,128)(2,1)S(1)}, u32[]{:S(2)}, u32[]{:S(2)}) collective-permute-start(bf16[64,2560]{1,0:T(8,128)(2,1)} %pack.1.refs_5_), channel_id=1, source_target_pairs={{0,2},{2,0},{4,6},{6,4},{8,10},{10,8},{12,14},{14,12},{16,18},{18,... | collective-permute-start | bytes 983048 | tf_op jit(solution)/shard_map/ppermute | solution.py:69
  6.2 1.5 collective-permute-start.3
  7.7 2.1 collective-permute-start.1
  9.8 2.6 %collective-permute-start = (bf16[64,2560]{1,0:T(8,128)(2,1)}, bf16[64,2560]{1,0:T(8,128)(2,1)S(1)}, u32[]{:S(2)}, u32[]{:S(2)}) collective-permute-start(bf16[64,2560]{1,0:T(8,128)(2,1)} %pack.1.refs_5_), channel_id=1, source_target_pairs={{0,16},{2,18},{4,20},{6,22},{8,24},{10,26},{12,28},{14,30},{16,0},... | collective-permute-start | bytes 983048 | tf_op jit(solution)/shard_map/ppermute | solution.py:69
  14.0 7.5 %norm_pixels.1 = (bf16[384,4096]{1,0:T(8,128)(2,1)}, f32[2,4096]{1,0:T(2,128)}) custom-call(f32[261,1,4096]{2,1,0:T(1,128)} %bitcast.30, f32[261,1]{1,0:T(8,128)} %copy.53.gain.refs_6_, f32[261,1]{1,0:T(8,128)} %copy.54.shift), custom_call_target="tpu_custom_call" | custom-call | flops 7699999744 | bytes 1024 | tf_op jit(solution)/shard_map/norm_pixels/pallas_call | solution.py:327
  23.8 2.5 %collective-permute-done.refs_0_ = bf16[64,2560]{1,0:T(8,128)(2,1)S(1)} collective-permute-done((bf16[64,2560]{1,0:T(8,128)(2,1)}, bf16[64,2560]{1,0:T(8,128)(2,1)S(1)}, u32[]{:S(2)}, u32[]{:S(2)}) %collective-permute-start) | collective-permute-done | bytes 327712 | tf_op jit(solution)/shard_map/ppermute | solution.py:69
  27.0 3.3 %stack.14 = (bf16[128,2560]{1,0:T(8,128)(2,1)}, bf16[128,2560]{1,0:T(8,128)(2,1)}, bf16[384,2560]{1,0:T(8,128)(2,1)}) custom-call(bf16[64,2560]{1,0:T(8,128)(2,1)} %copy-done.56, bf16[64,2560]{1,0:T(8,128)(2,1)} %copy-done.55, bf16[64,2560]{1,0:T(8,128)(2,1)} %copy-done.54, bf16[64,2560]{1,0:T(8,128)(2,1)} %copy-done.53, bf16[64,2560]{1,0:T(8,128)(2,1)} %copy-done.52, ...), custom_call_target="tpu_custom_call" | custom-call | flops 1650000000 | bytes 1024 | tf_op jit(solution)/shard_map/stack/pallas_call | solution.py:106
  30.7 1.5 collective-permute-start.10
  32.2 1.5 collective-permute-start.8
  33.8 2.4 %norm_latents.1.refs_3_.refs_14_.refs_17_ = bf16[256,1024]{1,0:T(8,128)(2,1)} custom-call(f32[256,1024]{1,0:T(8,128)} %bitcast.35, f32[6,1024]{1,0:T(8,128)} %refs_0_.1), custom_call_target="tpu_custom_call" | custom-call | flops 2200000000 | bytes 1024 | tf_op jit(solution)/shard_map/norm_latents/pallas_call | solution.py:345
  36.6 7.2 %collective-permute-done.6.refs_0_.refs_2_ = bf16[128,2560]{1,0:T(8,128)(2,1)S(1)} collective-permute-done((bf16[128,2560]{1,0:T(8,128)(2,1)}, bf16[128,2560]{1,0:T(8,128)(2,1)S(1)}, u32[]{:S(2)}, u32[]{:S(2)}) %collective-permute-start.6) | collective-permute-done | bytes 655392 | tf_op jit(solution)/shard_map/ppermute | solution.py:69
  43.9 1.5 collective-permute-done.10.refs_2_.refs_6_
  47.4 2.6 %stack.15 = (bf16[64,2560]{1,0:T(8,128)(2,1)}, bf16[64,2560]{1,0:T(8,128)(2,1)}, bf16[128,2560]{1,0:T(8,128)(2,1)}) custom-call(bf16[128,2560]{1,0:T(8,128)(2,1)} %copy-done.39, bf16[128,2560]{1,0:T(8,128)(2,1)} %copy-done.41, bf16[128,2560]{1,0:T(8,128)(2,1)} %copy-done.40, bf16[256,1024]{1,0:T(8,128)(2,1)} %norm_latents.1.refs_3_.refs_14_.refs_17_), custom_call_target="tpu_custom_call" | custom-call | flops 1650000000 | bytes 1024 | tf_op jit(solution)/shard_map/stack/pallas_call | solution.py:106
  52.3 1.5 collective-permute-start.14
  53.8 10.4 %collective-permute-done.12.refs_8_ = bf16[64,2560]{1,0:T(8,128)(2,1)S(1)} collective-permute-done((bf16[64,2560]{1,0:T(8,128)(2,1)}, bf16[64,2560]{1,0:T(8,128)(2,1)S(1)}, u32[]{:S(2)}, u32[]{:S(2)}) %collective-permute-start.12) | collective-permute-done | bytes 327712 | tf_op jit(solution)/shard_map/ppermute | solution.py:69
  65.3 1.4 collective-permute-done.11.refs_7_
  66.8 1.7 collective-permute-done.9.refs_5_
  70.8 1.3 copy-done.32
  72.1 15.3 %attend.1 = (bf16[512,1024]{1,0:T(8,128)(2,1)}, bf16[512,384]{1,0:T(8,128)(2,1)}, f32[512,384]{1,0:T(8,128)}) custom-call(s32[2]{0:T(128)} %pad_add_fusion.1.spot.refs_0_, bf16[384,2560]{1,0:T(8,128)(2,1)} %get-tuple-element.104.refs_0_, bf16[384,2560]{1,0:T(8,128)(2,1)} %copy-done.32, bf16[128,2560]{1,0:T(8,128)(2,1)} %copy-done.39, ...), custom_call_target="tpu_custom_call" | custom-call | flops 15399999488 | bytes 1024 | tf_op jit(solution)/shard_map/attend/pallas_call | solution.py:391
  87.7 2.3 %collective-permute-done.19.refs_15_ = f32[512,384]{1,0:T(8,128)S(1)} collective-permute-done((f32[512,384]{1,0:T(8,128)}, f32[512,384]{1,0:T(8,128)S(1)}, u32[]{:S(2)}, u32[]{:S(2)}) %collective-permute-start.19) | collective-permute-done | bytes 786464 | tf_op jit(solution)/shard_map/ppermute | solution.py:73
  90.9 19.9 %chain.1 = (f32[256,1024]{1,0:T(8,128)}, f32[256,1024]{1,0:T(8,128)}, bf16[512,384]{1,0:T(8,128)(2,1)}, f32[512,128]{1,0:T(8,128)}, f32[8,1024]{1,0:T(8,128)}, /...) custom-call(s32[2]{0:T(128)} %pad_add_fusion.1.spot.refs_0_, ...), custom_call_target="tpu_custom_call" | custom-call | flops 22000001024 | bytes 1024 | tf_op jit(solution)/shard_map/chain/pallas_call | solution.py:497
  111.8 1.6 collective-permute-start.23
  113.3 1.4 collective-permute-start.22
  115.4 12.1 %pixel_back.2 = (f32[512,384]{1,0:T(8,128)}, f32[261,128]{1,0:T(8,128)}, f32[261,1,4096]{2,1,0:T(1,128)}) custom-call(bf16[512,384]{1,0:T(8,128)(2,1)} %get-tuple-element.112.refs_0_, bf16[512,384]{1,0:T(8,128)(2,1)} %get-tuple-element.113.refs_1_, f32[512,128]{1,0:T(8,128)} %get-tuple-element.114.refs_2_, ...), custom_call_target="tpu_custom_call" | custom-call | flops 9900000256 | bytes 1024 | tf_op jit(solution)/shard_map/pixel_back/pallas_call | solution.py:593
  128.4 1.5 add_convert_fusion.1
  130.5 1.3 collective-permute-start.29
  131.8 12.4 %pixel_back.3 = (f32[512,384]{1,0:T(8,128)}, f32[261,128]{1,0:T(8,128)}, f32[261,1,4096]{2,1,0:T(1,128)}) custom-call(bf16[512,384]{1,0:T(8,128)(2,1)} %get-tuple-element.112.refs_0_, bf16[512,384]{1,0:T(8,128)(2,1)} %get-tuple-element.113.refs_1_, f32[512,128]{1,0:T(8,128)} %get-tuple-element.114.refs_2_, ...), custom_call_target="tpu_custom_call", output_to_operand_aliasing={{2}: (10, {})} | custom-call | flops 9900000256 | bytes 1024 | tf_op jit(solution)/shard_map/pixel_back/pallas_call | solution.py:593
  144.3 1.6 collective-permute-start.33
  145.9 1.4 collective-permute-start.34
  153.2 2.9 %collective-permute-start.30 = (bf16[64,1792]{1,0:T(8,128)(2,1)S(1)}, bf16[64,1792]{1,0:T(8,128)(2,1)S(1)}, u32[]{:S(2)}, u32[]{:S(2)}) collective-permute-start(bf16[64,1792]{1,0:T(8,128)(2,1)S(1)} %get-tuple-element.187), channel_id=1, source_target_pairs={{0,16},{2,18},{4,20},{6,22},{8,24},{10,26},{12,28},{14,30},{16,0},... | collective-permute-start | bytes 688136 | tf_op jit(solution)/shard_map/ppermute | solution.py:69
  157.0 8.6 %query_back.1 = (f32[256,1024]{1,0:T(8,128)}, f32[8,1024]{1,0:T(8,128)}, bf16[128,768]{1,0:T(8,128)(2,1)}, bf16[64,768]{1,0:T(8,128)(2,1)}, bf16[64,768]{1,0:T(8...) custom-call(s32[2]{0:T(128)} %pad_add_fusion.1.spot.refs_0_, ...), custom_call_target="tpu_custom_call" | custom-call | flops 9900000256 | bytes 1024 | tf_op jit(solution)/shard_map/query_back/pallas_call | solution.py:658
  168.0 1.5 collective-permute-start.38
  171.3 3.4 %collective-permute-done.37 = bf16[64,768]{1,0:T(8,128)(2,1)S(1)} collective-permute-done((bf16[64,768]{1,0:T(8,128)(2,1)}, bf16[64,768]{1,0:T(8,128)(2,1)S(1)}, u32[]{:S(2)}, u32[]{:S(2)}) %collective-permute-start.37) | collective-permute-done | bytes 98336 | tf_op jit(solution)/shard_map/ppermute | solution.py:69
  177.6 1.5 collective-permute-start.43
  179.1 1.4 collective-permute-start.44
  180.5 1.6 collective-permute-done.39
  182.9 2.6 %collective-permute-start.40 = (bf16[64,768]{1,0:T(8,128)(2,1)S(1)}, bf16[64,768]{1,0:T(8,128)(2,1)S(1)}, u32[]{:S(2)}, u32[]{:S(2)}) collective-permute-start(bf16[64,768]{1,0:T(8,128)(2,1)S(1)} %get-tuple-element.189), channel_id=1, source_target_pairs={{0,16},{2,18},{4,20},{6,22},{8,24},{10,26},{12,28},{14,30},{16,0},... | collective-permute-start | bytes 294920 | tf_op jit(solution)/shard_map/ppermute | solution.py:69
  186.9 2.7 %collective-permute-done.40 = bf16[64,768]{1,0:T(8,128)(2,1)S(1)} collective-permute-done((bf16[64,768]{1,0:T(8,128)(2,1)S(1)}, bf16[64,768]{1,0:T(8,128)(2,1)S(1)}, u32[]{:S(2)}, u32[]{:S(2)}) %collective-permute-start.40) | collective-permute-done | bytes 98336 | tf_op jit(solution)/shard_map/ppermute | solution.py:69
  190.2 1.9 collective-permute-done.42
  195.2 6.1 %moments.1 = (f32[4,64,1024]{2,1,0:T(8,128)}, f32[4,64,1024]{2,1,0:T(8,128)}, f32[4,64,1024]{2,1,0:T(8,128)}, f32[4,64,1024]{2,1,0:T(8,128)}, f32[2,64,261]{2,1,...) custom-call(s32[2]{0:T(128)} %pad_add_fusion.1.spot.refs_0_, ...), custom_call_target="tpu_custom_call" | custom-call | flops 5500000256 | bytes 1024 | tf_op jit(solution)/shard_map/moments/pallas_call | solution.py:716
  202.5 2.3 %collective-permute-start.48 = (f32[16,1024]{1,0:T(8,128)}, f32[16,1024]{1,0:T(8,128)S(1)}, u32[]{:S(2)}, u32[]{:S(2)}) collective-permute-start(f32[16,1024]{1,0:T(8,128)} %get-tuple-element.169), channel_id=1, source_target_pairs={{0,2},{2,0},{4,6},{6,4},{8,10},{10,8},{12,14},{14,12},{16,18},{18,... | collective-permute-start | bytes 196616 | tf_op jit(solution)/shard_map/ppermute | solution.py:69
  204.8 2.5 %collective-permute-done.50 = f32[16,1024]{1,0:T(8,128)S(1)} collective-permute-done((f32[16,1024]{1,0:T(8,128)}, f32[16,1024]{1,0:T(8,128)S(1)}, u32[]{:S(2)}, u32[]{:S(2)}) %collective-permute-start.50) | collective-permute-done | bytes 65568 | tf_op jit(solution)/shard_map/ppermute | solution.py:69
  208.2 2.2 collective-permute-start.53
  211.2 1.4 collective-permute-start.51
  212.6 2.3 %collective-permute-done.53 = f32[16,1024]{1,0:T(8,128)S(1)} collective-permute-done((f32[16,1024]{1,0:T(8,128)S(1)}, f32[16,1024]{1,0:T(8,128)S(1)}, u32[]{:S(2)}, u32[]{:S(2)}) %collective-permute-start.53) | collective-permute-done | bytes 65568 | tf_op jit(solution)/shard_map/ppermute | solution.py:69
  214.9 2.0 collective-permute-done.52
  217.6 3.3 %apply.1 = (f32[4,64,1024]{2,1,0:T(8,128)}, bf16[4,64,1024]{2,1,0:T(8,128)(2,1)}, f32[2,64,261]{2,1,0:T(8,128)}, bf16[2,64,261]{2,1,0:T(8,128)(2,1)}, f32[3,6]{1...) custom-call(f32[16,1024]{1,0:T(8,128)} %add_add_fusion.sums, ...), custom_call_target="tpu_custom_call" | custom-call | flops 4400000000 | bytes 1024 | tf_op jit(solution)/shard_map/apply/pallas_call | solution.py:757
  (221 shorter events, 41.3 us)
Async XLA Ops:
  3.3 18.2 %collective-permute-start.4 = (bf16[64,2560]{1,0:T(8,128)(2,1)}, bf16[64,2560]{1,0:T(8,128)(2,1)S(1)}, u32[]{:S(2)}, u32[]{:S(2)}) collective-permute-start(bf16[64,2560]{1,0:T(8,128)(2,1)} %pack.1.refs_5_), channel_id=1, source_target_pairs={{0,2},{2,0},{4,6},{6,4},{8,10},{10,8},{12,14},{14,12},{16,18},{18,... | collective-permute-start | bytes 983048 | tf_op jit(solution)/shard_map/ppermute | solution.py:69
  6.2 16.4 %collective-permute-start.3 = (bf16[64,2560]{1,0:T(8,128)(2,1)}, bf16[64,2560]{1,0:T(8,128)(2,1)S(1)}, u32[]{:S(2)}, u32[]{:S(2)}) collective-permute-start(bf16[64,2560]{1,0:T(8,128)(2,1)} %pack.1.refs_5_), channel_id=1, source_target_pairs={{0,4},{2,6},{4,0},{6,2},{8,12},{10,14},{12,8},{14,10},{16,20},{18,... | collective-permute-start | bytes 983048 | tf_op jit(solution)/shard_map/ppermute | solution.py:69
  7.7 14.9 %collective-permute-start.2 = (bf16[64,2560]{1,0:T(8,128)(2,1)}, bf16[64,2560]{1,0:T(8,128)(2,1)S(1)}, u32[]{:S(2)}, u32[]{:S(2)}) collective-permute-start(bf16[64,2560]{1,0:T(8,128)(2,1)} %pack.1.refs_5_), channel_id=1, source_target_pairs={{0,6},{2,4},{4,2},{6,0},{8,14},{10,12},{12,10},{14,8},{16,22},{18,... | collective-permute-start | bytes 983048 | tf_op jit(solution)/shard_map/ppermute | solution.py:69
  7.7 16.1 %collective-permute-start.1 = (bf16[64,2560]{1,0:T(8,128)(2,1)}, bf16[64,2560]{1,0:T(8,128)(2,1)S(1)}, u32[]{:S(2)}, u32[]{:S(2)}) collective-permute-start(bf16[64,2560]{1,0:T(8,128)(2,1)} %pack.1.refs_5_), channel_id=1, source_target_pairs={{0,8},{2,10},{4,12},{6,14},{8,0},{10,2},{12,4},{14,6},{16,24},{18,... | collective-permute-start | bytes 983048 | tf_op jit(solution)/shard_map/ppermute | solution.py:69
  9.8 16.5 %collective-permute-start = (bf16[64,2560]{1,0:T(8,128)(2,1)}, bf16[64,2560]{1,0:T(8,128)(2,1)S(1)}, u32[]{:S(2)}, u32[]{:S(2)}) collective-permute-start(bf16[64,2560]{1,0:T(8,128)(2,1)} %pack.1.refs_5_), channel_id=1, source_target_pairs={{0,16},{2,18},{4,20},{6,22},{8,24},{10,26},{12,28},{14,30},{16,0},... | collective-permute-start | bytes 983048 | tf_op jit(solution)/shard_map/ppermute | solution.py:69
  30.3 13.6 %collective-permute-start.6 = (bf16[128,2560]{1,0:T(8,128)(2,1)}, bf16[128,2560]{1,0:T(8,128)(2,1)S(1)}, u32[]{:S(2)}, u32[]{:S(2)}) collective-permute-start(bf16[128,2560]{1,0:T(8,128)(2,1)} %get-tuple-element.105), channel_id=1, source_target_pairs={{0,8},{2,10},{4,12},{6,14},{8,0},{10,2},{12,4},{14,6},{16,24},{18,... | collective-permute-start | bytes 1966088 | tf_op jit(solution)/shard_map/ppermute | solution.py:69
  30.7 14.6 %collective-permute-start.10 = (bf16[128,2560]{1,0:T(8,128)(2,1)}, bf16[128,2560]{1,0:T(8,128)(2,1)S(1)}, u32[]{:S(2)}, u32[]{:S(2)}) collective-permute-start(bf16[128,2560]{1,0:T(8,128)(2,1)} %get-tuple-element.106), channel_id=1, source_target_pairs={{0,2},{2,0},{4,6},{6,4},{8,10},{10,8},{12,14},{14,12},{16,18},{18,... | collective-permute-start | bytes 1966088 | tf_op jit(solution)/shard_map/ppermute | solution.py:69
  32.2 14.3 %collective-permute-start.8 = (bf16[128,2560]{1,0:T(8,128)(2,1)}, bf16[128,2560]{1,0:T(8,128)(2,1)S(1)}, u32[]{:S(2)}, u32[]{:S(2)}) collective-permute-start(bf16[128,2560]{1,0:T(8,128)(2,1)} %get-tuple-element.106), channel_id=1, source_target_pairs={{0,4},{2,6},{4,0},{6,2},{8,12},{10,14},{12,8},{14,10},{16,20},{18,... | collective-permute-start | bytes 1966088 | tf_op jit(solution)/shard_map/ppermute | solution.py:69
  33.8 37.0 %collective-permute-start.5 = (bf16[384,2560]{1,0:T(8,128)(2,1)}, bf16[384,2560]{1,0:T(8,128)(2,1)S(1)}, u32[]{:S(2)}, u32[]{:S(2)}) collective-permute-start(bf16[384,2560]{1,0:T(8,128)(2,1)} %get-tuple-element.104.refs_0_), channel_id=1, source_target_pairs={{0,1},{1,0},{2,3},{3,2},{4,5},{5,4},{6,7},{7,6},{8,9},{9,8},{10,11... | collective-permute-start | bytes 5898248 | tf_op jit(solution)/shard_map/ppermute | solution.py:73
  36.1 17.7 %collective-permute-start.18 = (bf16[256,1024]{1,0:T(8,128)(2,1)}, bf16[256,1024]{1,0:T(8,128)(2,1)S(1)}, u32[]{:S(2)}, u32[]{:S(2)}) collective-permute-start(bf16[256,1024]{1,0:T(8,128)(2,1)} %norm_latents.1.refs_3_.refs_14_.refs_17_), channel_id=1, source_target_pairs={{0,1},{1,0},{2,3},{3,2},{4,5},{5,4},{6,7},{7,6},{8,9},{9,8},{10,11... | collective-permute-start | bytes 1572872 | tf_op jit(solution)/shard_map/ppermute | solution.py:73
  50.0 14.3 %collective-permute-start.12 = (bf16[64,2560]{1,0:T(8,128)(2,1)}, bf16[64,2560]{1,0:T(8,128)(2,1)S(1)}, u32[]{:S(2)}, u32[]{:S(2)}) collective-permute-start(bf16[64,2560]{1,0:T(8,128)(2,1)} %get-tuple-element.107), channel_id=1, source_target_pairs={{0,16},{2,18},{4,20},{6,22},{8,24},{10,26},{12,28},{14,30},{16,0},... | collective-permute-start | bytes 983048 | tf_op jit(solution)/shard_map/ppermute | solution.py:69
  51.2 13.6 %collective-permute-start.16 = (bf16[128,2560]{1,0:T(8,128)(2,1)}, bf16[128,2560]{1,0:T(8,128)(2,1)S(1)}, u32[]{:S(2)}, u32[]{:S(2)}) collective-permute-start(bf16[128,2560]{1,0:T(8,128)(2,1)} %get-tuple-element.109), channel_id=1, source_target_pairs={{0,2},{2,0},{4,6},{6,4},{8,10},{10,8},{12,14},{14,12},{16,18},{18,... | collective-permute-start | bytes 1966088 | tf_op jit(solution)/shard_map/ppermute | solution.py:69
  52.3 12.0 %collective-permute-start.14 = (bf16[64,2560]{1,0:T(8,128)(2,1)}, bf16[64,2560]{1,0:T(8,128)(2,1)S(1)}, u32[]{:S(2)}, u32[]{:S(2)}) collective-permute-start(bf16[64,2560]{1,0:T(8,128)(2,1)} %get-tuple-element.108), channel_id=1, source_target_pairs={{0,4},{2,6},{4,0},{6,2},{8,12},{10,14},{12,8},{14,10},{16,20},{18,... | collective-permute-start | bytes 983048 | tf_op jit(solution)/shard_map/ppermute | solution.py:69
  53.8 11.0 %collective-permute-start.7 = (bf16[128,2560]{1,0:T(8,128)(2,1)}, bf16[128,2560]{1,0:T(8,128)(2,1)S(1)}, u32[]{:S(2)}, u32[]{:S(2)}) collective-permute-start(bf16[128,2560]{1,0:T(8,128)(2,1)} %copy-done.39), channel_id=1, source_target_pairs={{0,1},{1,0},{2,3},{3,2},{4,5},{5,4},{6,7},{7,6},{8,9},{9,8},{10,11... | collective-permute-start | bytes 1966088 | tf_op jit(solution)/shard_map/ppermute | solution.py:73
  64.3 4.2 %collective-permute-start.9 = (bf16[128,2560]{1,0:T(8,128)(2,1)}, bf16[128,2560]{1,0:T(8,128)(2,1)}, u32[]{:S(2)}, u32[]{:S(2)}) collective-permute-start(bf16[128,2560]{1,0:T(8,128)(2,1)} %copy-done.41), channel_id=1, source_target_pairs={{0,1},{1,0},{2,3},{3,2},{4,5},{5,4},{6,7},{7,6},{8,9},{9,8},{10,11... | collective-permute-start | bytes 1966088 | tf_op jit(solution)/shard_map/ppermute | solution.py:73
  64.8 4.4 %collective-permute-start.17 = (bf16[128,2560]{1,0:T(8,128)(2,1)S(1)}, bf16[128,2560]{1,0:T(8,128)(2,1)S(1)}, u32[]{:S(2)}, u32[]{:S(2)}) collective-permute-start(bf16[128,2560]{1,0:T(8,128)(2,1)S(1)} %collective-permute-done.16.refs_12_), channel_id=1, source_target_pairs={{0,1},{1,0},{2,3},{3,2},{4,5},{5,4},{6,7},{7,6},{8,9},{9,8},{10,11... | collective-permute-start | bytes 1966088 | tf_op jit(solution)/shard_map/ppermute | solution.py:73
  68.5 19.2 %collective-permute-start.20 = (f32[256,1024]{1,0:T(8,128)S(1)}, f32[256,1024]{1,0:T(8,128)S(1)}, u32[]{:S(2)}, u32[]{:S(2)}) collective-permute-start(f32[256,1024]{1,0:T(8,128)S(1)} %bitcast.38), channel_id=1, source_target_pairs={{0,1},{1,0},{2,3},{3,2},{4,5},{5,4},{6,7},{7,6},{8,9},{9,8},{10,11... | collective-permute-start | bytes 3145736 | tf_op jit(solution)/shard_map/ppermute | solution.py:73
  68.7 19.0 %collective-permute-start.21 = (f32[256,1024]{1,0:T(8,128)S(1)}, f32[256,1024]{1,0:T(8,128)S(1)}, u32[]{:S(2)}, u32[]{:S(2)}) collective-permute-start(f32[256,1024]{1,0:T(8,128)S(1)} %bitcast.34), channel_id=1, source_target_pairs={{0,1},{1,0},{2,3},{3,2},{4,5},{5,4},{6,7},{7,6},{8,9},{9,8},{10,11... | collective-permute-start | bytes 3145736 | tf_op jit(solution)/shard_map/ppermute | solution.py:73
  111.8 15.7 %collective-permute-start.23 = (bf16[64,1792]{1,0:T(8,128)(2,1)}, bf16[64,1792]{1,0:T(8,128)(2,1)S(1)}, u32[]{:S(2)}, u32[]{:S(2)}) collective-permute-start(bf16[64,1792]{1,0:T(8,128)(2,1)} %get-tuple-element.117), channel_id=1, source_target_pairs={{0,4},{2,6},{4,0},{6,2},{8,12},{10,14},{12,8},{14,10},{16,20},{18,... | collective-permute-start | bytes 688136 | tf_op jit(solution)/shard_map/ppermute | solution.py:69
  113.3 14.2 %collective-permute-start.24 = (bf16[64,1792]{1,0:T(8,128)(2,1)}, bf16[64,1792]{1,0:T(8,128)(2,1)S(1)}, u32[]{:S(2)}, u32[]{:S(2)}) collective-permute-start(bf16[64,1792]{1,0:T(8,128)(2,1)} %get-tuple-element.118), channel_id=1, source_target_pairs={{0,16},{2,18},{4,20},{6,22},{8,24},{10,26},{12,28},{14,30},{16,0},... | collective-permute-start | bytes 688136 | tf_op jit(solution)/shard_map/ppermute | solution.py:69
  113.3 14.2 %collective-permute-start.22 = (bf16[128,1792]{1,0:T(8,128)(2,1)}, bf16[128,1792]{1,0:T(8,128)(2,1)S(1)}, u32[]{:S(2)}, u32[]{:S(2)}) collective-permute-start(bf16[128,1792]{1,0:T(8,128)(2,1)} %get-tuple-element.116), channel_id=1, source_target_pairs={{0,2},{2,0},{4,6},{6,4},{8,10},{10,8},{12,14},{14,12},{16,18},{18,... | collective-permute-start | bytes 1376264 | tf_op jit(solution)/shard_map/ppermute | solution.py:69
  114.7 31.2 %collective-permute-start.27 = (bf16[128,1792]{1,0:T(8,128)(2,1)}, bf16[128,1792]{1,0:T(8,128)(2,1)S(1)}, u32[]{:S(2)}, u32[]{:S(2)}) collective-permute-start(bf16[128,1792]{1,0:T(8,128)(2,1)} %get-tuple-element.136), channel_id=1, source_target_pairs={{0,2},{2,0},{4,6},{6,4},{8,10},{10,8},{12,14},{14,12},{16,18},{18,... | collective-permute-start | bytes 1376264 | tf_op jit(solution)/shard_map/ppermute | solution.py:69
  129.9 17.4 %collective-permute-start.28 = (bf16[128,1792]{1,0:T(8,128)(2,1)S(1)}, bf16[128,1792]{1,0:T(8,128)(2,1)S(1)}, u32[]{:S(2)}, u32[]{:S(2)}) collective-permute-start(bf16[128,1792]{1,0:T(8,128)(2,1)S(1)} %pad_maximum_fusion), channel_id=1, source_target_pairs={{0,4},{2,6},{4,0},{6,2},{8,12},{10,14},{12,8},{14,10},{16,20},{18,... | collective-permute-start | bytes 1376264 | tf_op jit(solution)/shard_map/ppermute | solution.py:69
  130.5 16.8 %collective-permute-start.29 = (bf16[128,1792]{1,0:T(8,128)(2,1)S(1)}, bf16[128,1792]{1,0:T(8,128)(2,1)S(1)}, u32[]{:S(2)}, u32[]{:S(2)}) collective-permute-start(bf16[128,1792]{1,0:T(8,128)(2,1)S(1)} %pad_maximum_fusion.1), channel_id=1, source_target_pairs={{0,8},{2,10},{4,12},{6,14},{8,0},{10,2},{12,4},{14,6},{16,24},{18,... | collective-permute-start | bytes 1376264 | tf_op jit(solution)/shard_map/ppermute | solution.py:69
  144.2 11.9 %collective-permute-start.25 = (f32[512,384]{1,0:T(8,128)}, f32[512,384]{1,0:T(8,128)S(1)}, u32[]{:S(2)}, u32[]{:S(2)}) collective-permute-start(f32[512,384]{1,0:T(8,128)} %get-tuple-element.123.refs_14_.refs_3_), channel_id=1, source_target_pairs={{0,1},{1,0},{2,3},{3,2},{4,5},{5,4},{6,7},{7,6},{8,9},{9,8},{10,11... | collective-permute-start | bytes 2359304 | tf_op jit(solution)/shard_map/ppermute | solution.py:73
  144.3 21.4 %collective-permute-start.33 = (bf16[64,1792]{1,0:T(8,128)(2,1)}, bf16[64,1792]{1,0:T(8,128)(2,1)S(1)}, u32[]{:S(2)}, u32[]{:S(2)}) collective-permute-start(bf16[64,1792]{1,0:T(8,128)(2,1)} %get-tuple-element.147), channel_id=1, source_target_pairs={{0,4},{2,6},{4,0},{6,2},{8,12},{10,14},{12,8},{14,10},{16,20},{18,... | collective-permute-start | bytes 688136 | tf_op jit(solution)/shard_map/ppermute | solution.py:69
  145.9 19.8 %collective-permute-start.34 = (bf16[64,1792]{1,0:T(8,128)(2,1)S(1)}, bf16[64,1792]{1,0:T(8,128)(2,1)S(1)}, u32[]{:S(2)}, u32[]{:S(2)}) collective-permute-start(bf16[64,1792]{1,0:T(8,128)(2,1)S(1)} %copy-done.57), channel_id=1, source_target_pairs={{0,2},{2,0},{4,6},{6,4},{8,10},{10,8},{12,14},{14,12},{16,18},{18,... | collective-permute-start | bytes 688136 | tf_op jit(solution)/shard_map/ppermute | solution.py:69
  152.3 13.4 %collective-permute-start.31 = (bf16[64,1792]{1,0:T(8,128)(2,1)S(1)}, bf16[64,1792]{1,0:T(8,128)(2,1)S(1)}, u32[]{:S(2)}, u32[]{:S(2)}) collective-permute-start(bf16[64,1792]{1,0:T(8,128)(2,1)S(1)} %get-tuple-element.186), channel_id=1, source_target_pairs={{0,8},{2,10},{4,12},{6,14},{8,0},{10,2},{12,4},{14,6},{16,24},{18,... | collective-permute-start | bytes 688136 | tf_op jit(solution)/shard_map/ppermute | solution.py:69
  153.2 13.3 %collective-permute-start.30 = (bf16[64,1792]{1,0:T(8,128)(2,1)S(1)}, bf16[64,1792]{1,0:T(8,128)(2,1)S(1)}, u32[]{:S(2)}, u32[]{:S(2)}) collective-permute-start(bf16[64,1792]{1,0:T(8,128)(2,1)S(1)} %get-tuple-element.187), channel_id=1, source_target_pairs={{0,16},{2,18},{4,20},{6,22},{8,24},{10,26},{12,28},{14,30},{16,0},... | collective-permute-start | bytes 688136 | tf_op jit(solution)/shard_map/ppermute | solution.py:69
  156.1 10.3 %collective-permute-start.32 = (bf16[64,1792]{1,0:T(8,128)(2,1)S(1)}, bf16[64,1792]{1,0:T(8,128)(2,1)S(1)}, u32[]{:S(2)}, u32[]{:S(2)}) collective-permute-start(bf16[64,1792]{1,0:T(8,128)(2,1)S(1)} %get-tuple-element.188), channel_id=1, source_target_pairs={{0,6},{2,4},{4,2},{6,0},{8,14},{10,12},{12,10},{14,8},{16,22},{18,... | collective-permute-start | bytes 688136 | tf_op jit(solution)/shard_map/ppermute | solution.py:69
  167.3 8.0 %collective-permute-start.35 = (bf16[128,768]{1,0:T(8,128)(2,1)}, bf16[128,768]{1,0:T(8,128)(2,1)S(1)}, u32[]{:S(2)}, u32[]{:S(2)}) collective-permute-start(bf16[128,768]{1,0:T(8,128)(2,1)} %get-tuple-element.149), channel_id=1, source_target_pairs={{0,2},{2,0},{4,6},{6,4},{8,10},{10,8},{12,14},{14,12},{16,18},{18,... | collective-permute-start | bytes 589832 | tf_op jit(solution)/shard_map/ppermute | solution.py:69
  168.0 6.6 %collective-permute-start.37 = (bf16[64,768]{1,0:T(8,128)(2,1)}, bf16[64,768]{1,0:T(8,128)(2,1)S(1)}, u32[]{:S(2)}, u32[]{:S(2)}) collective-permute-start(bf16[64,768]{1,0:T(8,128)(2,1)} %get-tuple-element.151), channel_id=1, source_target_pairs={{0,16},{2,18},{4,20},{6,22},{8,24},{10,26},{12,28},{14,30},{16,0},... | collective-permute-start | bytes 294920 | tf_op jit(solution)/shard_map/ppermute | solution.py:69
  168.0 6.6 %collective-permute-start.38 = (bf16[64,768]{1,0:T(8,128)(2,1)}, bf16[64,768]{1,0:T(8,128)(2,1)S(1)}, u32[]{:S(2)}, u32[]{:S(2)}) collective-permute-start(bf16[64,768]{1,0:T(8,128)(2,1)} %get-tuple-element.152), channel_id=1, source_target_pairs={{0,4},{2,6},{4,0},{6,2},{8,12},{10,14},{12,8},{14,10},{16,20},{18,... | collective-permute-start | bytes 294920 | tf_op jit(solution)/shard_map/ppermute | solution.py:69
  169.7 10.9 %collective-permute-start.26 = (bf16[128,768]{1,0:T(8,128)(2,1)}, bf16[128,768]{1,0:T(8,128)(2,1)S(1)}, u32[]{:S(2)}, u32[]{:S(2)}) collective-permute-start(bf16[128,768]{1,0:T(8,128)(2,1)} %get-tuple-element.130.refs_8_), channel_id=1, source_target_pairs={{0,2},{2,0},{4,6},{6,4},{8,10},{10,8},{12,14},{14,12},{16,18},{18,... | collective-permute-start | bytes 589832 | tf_op jit(solution)/shard_map/ppermute | solution.py:69
  176.4 5.7 %collective-permute-start.39 = (bf16[128,768]{1,0:T(8,128)(2,1)S(1)}, bf16[128,768]{1,0:T(8,128)(2,1)S(1)}, u32[]{:S(2)}, u32[]{:S(2)}) collective-permute-start(bf16[128,768]{1,0:T(8,128)(2,1)S(1)} %pad_maximum_fusion.3), channel_id=1, source_target_pairs={{0,8},{2,10},{4,12},{6,14},{8,0},{10,2},{12,4},{14,6},{16,24},{18,... | collective-permute-start | bytes 589832 | tf_op jit(solution)/shard_map/ppermute | solution.py:69
  177.0 5.7 %collective-permute-start.36 = (bf16[128,768]{1,0:T(8,128)(2,1)S(1)}, bf16[128,768]{1,0:T(8,128)(2,1)S(1)}, u32[]{:S(2)}, u32[]{:S(2)}) collective-permute-start(bf16[128,768]{1,0:T(8,128)(2,1)S(1)} %pad_maximum_fusion.2), channel_id=1, source_target_pairs={{0,4},{2,6},{4,0},{6,2},{8,12},{10,14},{12,8},{14,10},{16,20},{18,... | collective-permute-start | bytes 589832 | tf_op jit(solution)/shard_map/ppermute | solution.py:69
  177.6 9.2 %collective-permute-start.43 = (bf16[64,768]{1,0:T(8,128)(2,1)}, bf16[64,768]{1,0:T(8,128)(2,1)S(1)}, u32[]{:S(2)}, u32[]{:S(2)}) collective-permute-start(bf16[64,768]{1,0:T(8,128)(2,1)} %get-tuple-element.155), channel_id=1, source_target_pairs={{0,4},{2,6},{4,0},{6,2},{8,12},{10,14},{12,8},{14,10},{16,20},{18,... | collective-permute-start | bytes 294920 | tf_op jit(solution)/shard_map/ppermute | solution.py:69
  179.1 7.8 %collective-permute-start.44 = (bf16[64,768]{1,0:T(8,128)(2,1)}, bf16[64,768]{1,0:T(8,128)(2,1)S(1)}, u32[]{:S(2)}, u32[]{:S(2)}) collective-permute-start(bf16[64,768]{1,0:T(8,128)(2,1)} %get-tuple-element.156), channel_id=1, source_target_pairs={{0,2},{2,0},{4,6},{6,4},{8,10},{10,8},{12,14},{14,12},{16,18},{18,... | collective-permute-start | bytes 294920 | tf_op jit(solution)/shard_map/ppermute | solution.py:69
  182.9 6.7 %collective-permute-start.40 = (bf16[64,768]{1,0:T(8,128)(2,1)S(1)}, bf16[64,768]{1,0:T(8,128)(2,1)S(1)}, u32[]{:S(2)}, u32[]{:S(2)}) collective-permute-start(bf16[64,768]{1,0:T(8,128)(2,1)S(1)} %get-tuple-element.189), channel_id=1, source_target_pairs={{0,16},{2,18},{4,20},{6,22},{8,24},{10,26},{12,28},{14,30},{16,0},... | collective-permute-start | bytes 294920 | tf_op jit(solution)/shard_map/ppermute | solution.py:69
  185.5 4.6 %collective-permute-start.41 = (bf16[64,768]{1,0:T(8,128)(2,1)S(1)}, bf16[64,768]{1,0:T(8,128)(2,1)S(1)}, u32[]{:S(2)}, u32[]{:S(2)}) collective-permute-start(bf16[64,768]{1,0:T(8,128)(2,1)S(1)} %get-tuple-element.190), channel_id=1, source_target_pairs={{0,8},{2,10},{4,12},{6,14},{8,0},{10,2},{12,4},{14,6},{16,24},{18,... | collective-permute-start | bytes 294920 | tf_op jit(solution)/shard_map/ppermute | solution.py:69
  186.6 5.5 %collective-permute-start.42 = (bf16[64,768]{1,0:T(8,128)(2,1)S(1)}, bf16[64,768]{1,0:T(8,128)(2,1)S(1)}, u32[]{:S(2)}, u32[]{:S(2)}) collective-permute-start(bf16[64,768]{1,0:T(8,128)(2,1)S(1)} %get-tuple-element.194), channel_id=1, source_target_pairs={{0,6},{2,4},{4,2},{6,0},{8,14},{10,12},{12,10},{14,8},{16,22},{18,... | collective-permute-start | bytes 294920 | tf_op jit(solution)/shard_map/ppermute | solution.py:69
  186.8 7.5 %collective-permute-start.46 = (f32[64,1792]{1,0:T(8,128)S(1)}, f32[64,1792]{1,0:T(8,128)S(1)}, u32[]{:S(2)}, u32[]{:S(2)}) collective-permute-start(f32[64,1792]{1,0:T(8,128)S(1)} %convert_add_fusion.refs_3_), channel_id=1, source_target_pairs={{0,1},{1,0},{2,3},{3,2},{4,5},{5,4},{6,7},{7,6},{8,9},{9,8},{10,11... | collective-permute-start | bytes 1376264 | tf_op jit(solution)/shard_map/ppermute | solution.py:73
  201.3 6.0 %collective-permute-start.50 = (f32[16,1024]{1,0:T(8,128)}, f32[16,1024]{1,0:T(8,128)S(1)}, u32[]{:S(2)}, u32[]{:S(2)}) collective-permute-start(f32[16,1024]{1,0:T(8,128)} %get-tuple-element.169), channel_id=1, source_target_pairs={{0,6},{2,4},{4,2},{6,0},{8,14},{10,12},{12,10},{14,8},{16,22},{18,... | collective-permute-start | bytes 196616 | tf_op jit(solution)/shard_map/ppermute | solution.py:69
  201.3 6.0 %collective-permute-start.49 = (f32[16,1024]{1,0:T(8,128)}, f32[16,1024]{1,0:T(8,128)S(1)}, u32[]{:S(2)}, u32[]{:S(2)}) collective-permute-start(f32[16,1024]{1,0:T(8,128)} %get-tuple-element.169), channel_id=1, source_target_pairs={{0,4},{2,6},{4,0},{6,2},{8,12},{10,14},{12,8},{14,10},{16,20},{18,... | collective-permute-start | bytes 196616 | tf_op jit(solution)/shard_map/ppermute | solution.py:69
  202.5 4.8 %collective-permute-start.48 = (f32[16,1024]{1,0:T(8,128)}, f32[16,1024]{1,0:T(8,128)S(1)}, u32[]{:S(2)}, u32[]{:S(2)}) collective-permute-start(f32[16,1024]{1,0:T(8,128)} %get-tuple-element.169), channel_id=1, source_target_pairs={{0,2},{2,0},{4,6},{6,4},{8,10},{10,8},{12,14},{14,12},{16,18},{18,... | collective-permute-start | bytes 196616 | tf_op jit(solution)/shard_map/ppermute | solution.py:69
  208.2 6.8 %collective-permute-start.53 = (f32[16,1024]{1,0:T(8,128)S(1)}, f32[16,1024]{1,0:T(8,128)S(1)}, u32[]{:S(2)}, u32[]{:S(2)}) collective-permute-start(f32[16,1024]{1,0:T(8,128)S(1)} %add_add_fusion.1), channel_id=1, source_target_pairs={{0,24},{2,26},{4,28},{6,30},{8,16},{10,18},{12,20},{14,22},{16,8},... | collective-permute-start | bytes 196616 | tf_op jit(solution)/shard_map/ppermute | solution.py:69
  210.3 6.7 %collective-permute-start.52 = (f32[16,1024]{1,0:T(8,128)S(1)}, f32[16,1024]{1,0:T(8,128)S(1)}, u32[]{:S(2)}, u32[]{:S(2)}) collective-permute-start(f32[16,1024]{1,0:T(8,128)S(1)} %add_add_fusion.1), channel_id=1, source_target_pairs={{0,16},{2,18},{4,20},{6,22},{8,24},{10,26},{12,28},{14,30},{16,0},... | collective-permute-start | bytes 196616 | tf_op jit(solution)/shard_map/ppermute | solution.py:69
  211.2 5.8 %collective-permute-start.51 = (f32[16,1024]{1,0:T(8,128)S(1)}, f32[16,1024]{1,0:T(8,128)S(1)}, u32[]{:S(2)}, u32[]{:S(2)}) collective-permute-start(f32[16,1024]{1,0:T(8,128)S(1)} %add_add_fusion.1), channel_id=1, source_target_pairs={{0,8},{2,10},{4,12},{6,14},{8,0},{10,2},{12,4},{14,6},{16,24},{18,... | collective-permute-start | bytes 196616 | tf_op jit(solution)/shard_map/ppermute | solution.py:69
  (65 other events, 501.5 us)
